TPU v7x, 32 devices: a whole 2x2x4 slice. The times are simulated.
32 devices in a mesh: ctx: 8 (over y, x, core), head: 4 (over z).
Axes of the slice: x: 2, y: 2, z: 4, core: 2. Of those that a mesh axis runs over, the one named last changes fastest.
Arguments:
- query_heads: bfloat16 [128, 128, 192], P('ctx', 'head'), may hold values from -6 to 6
- absorb_up: bfloat16 [128, 128, 512], P('head'), may hold values from -0.5 to 0.5
- latent_keys: bfloat16 [8192, 576], P('ctx'), may hold values from -6 to 6
- lse_heads: float32 [128, 128], P(None, 'head'), as said below
- index_query: bfloat16 [128, 64, 128], P('ctx', 'head'), may hold values from -6 to 6
- index_weight: bfloat16 [128, 64], P('ctx', 'head'), may hold values from -0.75 to 0.75
- index_keys: bfloat16 [8192, 128], P('ctx'), may hold values from -6 to 6
- lse_index: float32 [128], replicated, as said below
- query_pos: int32 [128], replicated, may hold values from 0 to 8191, as said below
- key_blocks: int32 [8], P('ctx'), may hold values from 0 to 7, each once
Outputs:
- query_grad: float32 [128, 64, 128], P('ctx', 'head')
- key_grad: float32 [8192, 128], P(('ctx', 'head'))
Inputs may be any that keep to these rules, and one draw needn't show every extreme that they name: `query_pos`: positions of the queries in a causal sequence of 8192 tokens. `key_blocks`: each index of ctx holds the 1024 keys of one block of the sequence, every block once. `lse_heads`: saved log-sum-exp values of the attention heads. `lse_index`: saved log normalizers of the indexer.
All inputs are finite; a program needn't handle non-finite values.
Results may differ from a plain program's by a relative error of at most 0.0094.
Values may be sent and summed in bfloat16 or wider, within the bound.
No kernel may reach another device: no remote copies, remote signals or barrier semaphores. Data moves between devices by JAX's collectives and lax.ppermute only.
A program may use at most 64 MiB of HBM per device.

v0:
```python
import jax
import jax.numpy as jnp
from jax import lax
from jax.sharding import PartitionSpec as P

DN = 128
DI = 128
DQ = 192


def absorb(raw_heads, absorb_up):
    nope_part = jnp.einsum(
        "rhn,hnc->rhc", raw_heads[:, :, :DN], absorb_up, preferred_element_type=jnp.float32
    ).astype(jnp.bfloat16)
    return jnp.concatenate([nope_part, raw_heads[:, :, DN:]], axis=2)


def head_probs(absorbed, latent_keys, lse_heads, visible, attn_scale):
    row_count = absorbed.shape[0]
    local_heads = absorbed.shape[1]
    group_size = min(8, local_heads)

    def add_group(step_index, running):
        first_head = step_index * group_size
        query_group = lax.dynamic_slice_in_dim(absorbed, first_head, group_size, 1)
        lse_group = lax.dynamic_slice_in_dim(lse_heads, first_head, group_size, 1)
        scores = (
            jnp.einsum("rgc,kc->rgk", query_group, latent_keys, preferred_element_type=jnp.float32)
            * attn_scale
        )
        prob_rows = jnp.where(visible[:, None, :], jnp.exp(scores - lse_group[:, :, None]), 0.0)
        return running + jnp.sum(prob_rows, axis=1)

    initial = jnp.zeros((row_count, latent_keys.shape[0]), jnp.float32)
    return lax.fori_loop(0, local_heads // group_size, add_group, initial)


def body(
    query_heads,
    absorb_up,
    latent_keys,
    lse_heads,
    index_query,
    index_weight,
    index_keys,
    lse_index,
    query_pos,
    key_blocks,
):
    key_count = latent_keys.shape[0]
    key_pos = key_blocks[0] * key_count + jnp.arange(key_count, dtype=jnp.int32)
    visible = key_pos[None, :] <= query_pos[:, None]
    attn_scale = DQ ** (-0.5)
    prob_part = head_probs(
        absorb(lax.all_gather(query_heads, "ctx", axis=0, tiled=True), absorb_up),
        latent_keys,
        lse_heads,
        visible,
        attn_scale,
    )
    all_query, all_weight = (
        lax.all_gather(index_query, "ctx", axis=0, tiled=True),
        lax.all_gather(index_weight, "ctx", axis=0, tiled=True),
    )
    index_scale = DI ** (-0.5)
    index_score = (
        jnp.einsum("qjd,kd->qjk", all_query, index_keys, preferred_element_type=jnp.float32)
        * index_scale
    )
    weight_float = all_weight.astype(jnp.float32)
    logit_part = jnp.sum(weight_float[:, :, None] * jax.nn.relu(index_score), axis=1)
    loss_scale = (key_count * lax.axis_size("ctx")) ** 0.5
    prob_sum, logit_sum = lax.psum((prob_part, logit_part), "head")
    row_total = lax.psum(jnp.sum(prob_sum, axis=1), "ctx")
    index_prob = jnp.where(visible, jnp.exp(logit_sum - lse_index[:, None]), 0.0)
    d_logit = loss_scale * (index_prob - prob_sum / row_total[:, None])
    d_score = jnp.where(
        index_score > 0.0, weight_float[:, :, None] * d_logit[:, None, :], 0.0
    ).astype(jnp.bfloat16)
    query_grad = lax.psum_scatter(
        jnp.einsum("qjk,kd->qjd", d_score, index_keys, preferred_element_type=jnp.float32)
        * index_scale,
        "ctx",
        scatter_dimension=0,
        tiled=True,
    )
    key_part = (
        jnp.einsum("qjk,qjd->kd", d_score, all_query, preferred_element_type=jnp.float32)
        * index_scale
    )
    key_grad = lax.psum_scatter(key_part, "head", scatter_dimension=0, tiled=True)
    return (query_grad, key_grad)


def solution(mesh):
    placed = (
        P("ctx", "head", None),
        P("head", None, None),
        P("ctx", None),
        P(None, "head"),
        P("ctx", "head", None),
        P("ctx", "head"),
        P("ctx", None),
        P(),
        P(),
        P("ctx"),
    )
    return jax.shard_map(
        body,
        mesh=mesh,
        in_specs=placed,
        out_specs=(P("ctx", "head", None), P(("ctx", "head"), None)),
        check_vma=False,
    )
```

profile of v0, /device:TPU:0, one launch (start us, length us, event | category | flops | bytes accessed | tf_op | source)
XLA Modules:
  0.0 206.2 jit_solution(13352368776782373441)
XLA Ops:
  7.2 0.0 copy-start
  7.2 0.0 all-gather.2.cloned.1.call-start
  7.2 1.9 copy.28
  9.1 0.0 all-gather.2.cloned.1.call-update
  9.1 0.0 all-reduce.3.cloned.1.call-start
  9.8 10.7 %all_gather.10 = bf16[128,16]{1,0:T(8,128)(2,1)S(1)} all-gather(bf16[16,16]{1,0:T(8,128)(2,1)} %param.17), channel_id=1, replica_groups=mesh['ctx'=8,'head'=4] {'ctx'}, dimensions={0}, use_global_device_ids=true | all-gather | bytes 4608 | tf_op jit(solution)/shard_map/all_gather | solution.py:63
  20.5 0.1 copy.27
  20.5 0.9 copy.26
  21.4 11.2 %all_gather.9 = bf16[128,16,128]{2,0,1:T(8,128)(2,1)S(1)} all-gather(bf16[16,16,128]{2,0,1:T(8,128)(2,1)S(1)} %copy.26), channel_id=1, replica_groups=mesh['ctx'=8,'head'=4] {'ctx'}, dimensions={0}, use_global_device_ids=true | all-gather | bytes 589824 | tf_op jit(solution)/shard_map/all_gather | solution.py:62
  32.7 4.8 %multiply_reduce_fusion = (f32[128,1024]{1,0:T(8,128)}, f32[128,16,1024]{2,0,1:T(8,128)}) fusion(f32[128,16]{0,1:T(8,128)S(1)} %convert_element_type.12, bf16[128,16,128]{2,0,1:T(8,128)(2,1)S(1)} %all_gather.9, bf16[1024,128]{1,0:T(8,128)(2,1)S(1)} %copy-done), kind=kOutput, calls=%fused_computation.11 | convolution fusion | flops 545128448 | bytes 9707520 | tf_op jit(solution)/shard_map/qjd,kd->qjk/dot_general | solution.py:67
  37.5 3.3 %all-gather.2.cloned.1.call-done = bf16[128,32,192]{2,0,1:T(8,128)(2,1)} async-done(((bf16[16,32,192]{2,0,1:T(8,128)(2,1)}), bf16[128,32,192]{2,0,1:T(8,128)(2,1)}) %all-gather.2.cloned.1.call-update) | async-done | bytes 1572880 | tf_op jit(solution)/shard_map/all_gather | solution.py:55
  40.8 1.3 slice.9
  42.1 0.4 copy.30
  42.5 3.8 %convert_bitcast_fusion = bf16[128,32,512]{0,2,1:T(8,128)(2,1)S(1)} fusion(bf16[32,128,512]{2,1,0:T(8,128)(2,1)} %param.13, bf16[128,32,192]{2,0,1:T(8,128)(2,1)} %all-gather.2.cloned.1.call-done), kind=kOutput, calls=%fused_computation.20 | convolution fusion | flops 538968064 | bytes 9437184 | tf_op jit(solution)/shard_map/rhn,hnc->rhc/dot_general | solution.py:12
  46.3 2.5 %pad_maximum_fusion = bf16[128,32,576]{0,2,1:T(8,128)(2,1)} fusion(bf16[128,32,64]{0,2,1:T(8,128)(2,1)S(1)} %copy.30, bf16[128,32,512]{0,2,1:T(8,128)(2,1)S(1)} %convert_bitcast_fusion), kind=kLoop, calls=%fused_computation.12 | loop fusion | flops 9437184 | bytes 9437184 | tf_op jit(solution)/shard_map/concatenate | solution.py:15
  48.8 20.7 %while.14 = (s32[]{:T(128)}, f32[128,1024]{1,0:T(8,128)S(1)}, bf16[128,32,576]{0,2,1:T(8,128)(2,1)}, bf16[1024,576]{0,1:T(8,128)(2,1)}, f32[128,32]{0,1:T(8,128)...) while((s32[]{:T(128)}, f32[128,1024]{1,0:T(8,128)S(1)}, ...), condition=%wide.region_4.5_spmd.clone, body=%wide.region_2.0_spmd.clone.sunk | while | flops 1212416000 | bytes 4735669 | solution.py:35
  48.8 0.7 constant_dynamic-slice_fusion.2
  49.5 0.1 broadcast_compare_fusion.2
  49.6 4.1 %select_reduce_fusion.2 = f32[128,1024]{1,0:T(8,128)S(1)} fusion(f32[128,8]{0,1:T(8,128)S(1)} %constant_dynamic-slice_fusion.2, pred[128,1024]{1,0:T(8,128)(4,1)S(1)} %broadcast_compare_fusion.2, bf16[1024,576]{0,1:T(8,128)(2,1)} %get-tuple-element.232, bf16[128,32,576]{0,2,1:T(8,128)(2,1)} %get-tuple-element.231, s32[]{:T(128)S(6)} %select_n.42), kind=kOutput, calls=%fused_computation.1.clone.1 | convolution fusion | flops 1212022784 | bytes 3018756 | tf_op jit(solution)/shard_map/while/body/eval_jaxpr/rgc,kc->rgk/dot_general | solution.py:28
  53.8 0.2 select_add_fusion.2
  54.0 0.7 constant_dynamic-slice_fusion.2
  54.7 0.1 broadcast_compare_fusion.2
  54.8 4.1 %select_reduce_fusion.2 = f32[128,1024]{1,0:T(8,128)S(1)} fusion(f32[128,8]{0,1:T(8,128)S(1)} %constant_dynamic-slice_fusion.2, pred[128,1024]{1,0:T(8,128)(4,1)S(1)} %broadcast_compare_fusion.2, bf16[1024,576]{0,1:T(8,128)(2,1)} %get-tuple-element.232, bf16[128,32,576]{0,2,1:T(8,128)(2,1)} %get-tuple-element.231, s32[]{:T(128)S(6)} %select_n.42), kind=kOutput, calls=%fused_computation.1.clone.1 | convolution fusion | flops 1212022784 | bytes 3018756 | tf_op jit(solution)/shard_map/while/body/eval_jaxpr/rgc,kc->rgk/dot_general | solution.py:28
  59.0 0.2 select_add_fusion.2
  59.2 0.7 constant_dynamic-slice_fusion.2
  59.9 0.1 broadcast_compare_fusion.2
  60.0 4.1 %select_reduce_fusion.2 = f32[128,1024]{1,0:T(8,128)S(1)} fusion(f32[128,8]{0,1:T(8,128)S(1)} %constant_dynamic-slice_fusion.2, pred[128,1024]{1,0:T(8,128)(4,1)S(1)} %broadcast_compare_fusion.2, bf16[1024,576]{0,1:T(8,128)(2,1)} %get-tuple-element.232, bf16[128,32,576]{0,2,1:T(8,128)(2,1)} %get-tuple-element.231, s32[]{:T(128)S(6)} %select_n.42), kind=kOutput, calls=%fused_computation.1.clone.1 | convolution fusion | flops 1212022784 | bytes 3018756 | tf_op jit(solution)/shard_map/while/body/eval_jaxpr/rgc,kc->rgk/dot_general | solution.py:28
  64.2 0.2 select_add_fusion.2
  64.4 0.7 constant_dynamic-slice_fusion.2
  65.1 0.1 broadcast_compare_fusion.2
  65.2 4.1 %select_reduce_fusion.2 = f32[128,1024]{1,0:T(8,128)S(1)} fusion(f32[128,8]{0,1:T(8,128)S(1)} %constant_dynamic-slice_fusion.2, pred[128,1024]{1,0:T(8,128)(4,1)S(1)} %broadcast_compare_fusion.2, bf16[1024,576]{0,1:T(8,128)(2,1)} %get-tuple-element.232, bf16[128,32,576]{0,2,1:T(8,128)(2,1)} %get-tuple-element.231, s32[]{:T(128)S(6)} %select_n.42), kind=kOutput, calls=%fused_computation.1.clone.1 | convolution fusion | flops 1212022784 | bytes 3018756 | tf_op jit(solution)/shard_map/while/body/eval_jaxpr/rgc,kc->rgk/dot_general | solution.py:28
  69.3 0.2 select_add_fusion.2
  69.5 0.8 copy-done.1
  70.3 0.0 all-reduce.3.cloned.1.call-update
  70.4 0.0 reduce-scatter.3.cloned.1.call-start
  70.4 4.8 %fusion.7 = u16[128,1024]{1,0:T(8,128)(2,1)S(1)} fusion(f32[128,16,1024]{2,0,1:T(8,128)} %get-tuple-element.163), kind=kLoop, calls=%fused_computation.15 | loop fusion | flops 12451840 | bytes 8650752
  75.2 47.5 %all-reduce.3.cloned.1.call-done = (f32[128,1024]{1,0:T(8,128)}, f32[128,1024]{1,0:T(8,128)}) async-done(((f32[128,1024]{1,0:T(8,128)}, f32[128,1024]{1,0:T(8,128)}), (f32[128,1024]{1,0:T(8,128)}, f32[128,1024]{1,0:T(8,128)})) %all-reduce.3.cloned.1.call-update) | async-done | bytes 1048592 | tf_op jit(solution)/shard_map/psum | solution.py:73
  122.7 1.2 reduce_sum.32
  123.8 13.8 %psum.23 = f32[128]{0:T(128)S(1)} all-reduce(f32[128]{0:T(128)S(1)} %reduce_sum.32), channel_id=1, replica_groups=mesh['ctx'=8,'head'=4] {'ctx'}, use_global_device_ids=true, to_apply=%region_7.8 | all-reduce | flops 128 | bytes 1024 | tf_op jit(solution)/shard_map/psum | solution.py:74
  137.7 1.4 subtract_multiply_fusion
  139.1 2.4 %fusion.18 = f32[128,16,128]{2,0,1:T(8,128)} fusion(f32[128,1024]{1,0:T(8,128)S(1)} %subtract_multiply_fusion, f32[128,16]{0,1:T(8,128)S(1)} %convert_element_type.12, u16[128,1024]{1,0:T(8,128)(2,1)S(1)} %fusion.7, bf16[1024,128]{1,0:T(8,128)(2,1)S(1)} %copy-done), kind=kOutput, calls=%fused_computation.27 | convolution fusion | flops 551813120 | bytes 2105344 | tf_op jit(solution)/shard_map/qjk,kd->qjd/dot_general | solution.py:81
  141.5 0.0 reduce-scatter.3.cloned.1.call-update
  141.5 0.0 reduce-scatter.5.cloned.1.call-start
  141.5 2.6 %fusion.20 = f32[1024,128]{1,0:T(8,128)} fusion(bf16[128,16,128]{2,0,1:T(8,128)(2,1)S(1)} %all_gather.9, f32[128,1024]{1,0:T(8,128)S(1)} %subtract_multiply_fusion, f32[128,16]{0,1:T(8,128)S(1)} %convert_element_type.12, u16[128,1024]{1,0:T(8,128)(2,1)S(1)} %fusion.7), kind=kOutput, calls=%fused_computation.29 | convolution fusion | flops 551682048 | bytes 1843200 | tf_op jit(solution)/shard_map/qjk,qjd->kd/dot_general | solution.py:88
  144.1 0.0 reduce-scatter.5.cloned.1.call-update
  144.1 31.1 %reduce-scatter.3.cloned.1.call-done = f32[16,16,128]{2,0,1:T(8,128)} async-done(((f32[128,16,128]{2,0,1:T(8,128)}), f32[16,16,128]{2,0,1:T(8,128)}) %reduce-scatter.3.cloned.1.call-update) | async-done | bytes 131088 | tf_op jit(solution)/shard_map/reduce_scatter | solution.py:80
  175.2 1.6 copy.32
  176.8 22.8 %reduce-scatter.5.cloned.1.call-done = f32[256,128]{1,0:T(8,128)} async-done(((f32[1024,128]{1,0:T(8,128)}), f32[256,128]{1,0:T(8,128)}) %reduce-scatter.5.cloned.1.call-update) | async-done | bytes 131088 | tf_op jit(solution)/shard_map/reduce_scatter | solution.py:91
  (9 shorter events, 0.0 us)
Async XLA Ops:
  7.2 25.5 %copy-start = (bf16[1024,128]{1,0:T(8,128)(2,1)S(1)}, bf16[1024,128]{1,0:T(8,128)(2,1)}, u32[]{:S(2)}) copy-start(bf16[1024,128]{1,0:T(8,128)(2,1)} %param.18) | copy-start | bytes 786436
  7.2 33.6 %all-gather.2.cloned.1.call-start = ((), (), s32[]{:S(2)}) async-start(), calls=%async_computation.2 | async-start | bytes 2359296 | tf_op jit(solution)/shard_map/all_gather | solution.py:55
  9.1 113.6 %all-reduce.3.cloned.1.call-start = ((), (), s32[]{:S(2)}) async-start(), calls=%async_computation.5 | async-start | bytes 2097152 | tf_op jit(solution)/shard_map/psum | solution.py:73
  46.3 2.5 %copy-start.2 = (s32[128]{0:T(128)S(1)}, s32[128]{0:T(128)}, u32[]{:S(2)}) copy-start(s32[128]{0:T(128)} %param.20) | copy-start | bytes 1540
  69.5 0.8 copy-start.1
  70.4 67.3 %copy-start.3 = (f32[128]{0:T(128)S(1)}, f32[128]{0:T(128)}, u32[]{:S(2)}) copy-start(f32[128]{0:T(128)} %param.19) | copy-start | bytes 1540
  70.4 104.8 %reduce-scatter.3.cloned.1.call-start = ((), (), s32[]{:S(2)}) async-start(), calls=%async_computation.3 | async-start | bytes 1179648 | tf_op jit(solution)/shard_map/reduce_scatter | solution.py:80
  141.5 58.2 %reduce-scatter.5.cloned.1.call-start = ((), (), s32[]{:S(2)}) async-start(), calls=%async_computation.4 | async-start | bytes 655360 | tf_op jit(solution)/shard_map/reduce_scatter | solution.py:91
Sparse Core Ops, SparseCore 0:
  9.9 30.8 all-gather.1
  70.5 52.1 all-reduce.2
  141.6 33.5 reduce-scatter.2
  178.0 21.5 reduce-scatter.4
where the time goes:
time: 207 us; the launch traced here: 206 us
  waiting for transfers between devices  105 us (51%)
  blocking collectives  35.7 us (17%)
  matrix products  30.2 us (15%)
  between operations  14.5 us (7%)
  other arithmetic  11.1 us (5%)
  local copies, waits for them, and re-layouts  9.65 us (5%)
    psum x1, waiting for transfers between devices, body(): prob_sum, logit_sum = lax.psum((prob_part, logit_part), 'head')  47.5 us
    reduce_scatter x1, waiting for transfers between devices, body(): lax.psum_scatter(jnp.einsum('qjk,kd->qjd', d_score, index_keys, preferred...  31.1 us
    reduce_scatter x1, waiting for transfers between devices, body(): lax.psum_scatter(key_part, 'head', scatter_dimension=0, tiled=True)  22.8 us
    dot_general x4, matrix products, add_group(): jnp.einsum('rgc,kc->rgk', query_group, latent_keys, preferred_element_typ...  16.5 us
    psum x1, blocking collectives, body(): row_total = lax.psum(jnp.sum(prob_sum, axis=1), 'ctx')  13.8 us
    all_gather x1, blocking collectives, body(): lax.all_gather(index_query, 'ctx', axis=0, tiled=True)  11.2 us
    all_gather x1, blocking collectives, body(): lax.all_gather(index_weight, 'ctx', axis=0, tiled=True)  10.7 us
    unnamed x11, local copies, waits for them, and re-layouts  5.15 us
  transfers between devices with their start and end apart: 4, of which 4 were waited for; matrix products, arithmetic and copies ran while one was open for 7% of the time, Pallas kernels for 0%

commit v1 on v0

v1 whole, which is shorter than its diff:
```python
import functools
import math

import jax
import jax.numpy as jnp
from jax import lax
from jax.experimental import pallas as pl
from jax.experimental.pallas import tpu as pltpu
from jax.sharding import PartitionSpec as P

LOG2E = math.log2(math.e)
F32 = jnp.float32
BF16 = jnp.bfloat16
LANES = 128
VMEM_LIMIT = 48 * 1024 * 1024


def matmul(lhs, rhs):
    return jnp.dot(lhs, rhs, preferred_element_type=F32)


def send(array, axis, size, offset):
    return lax.ppermute(array, axis, [(i, i ^ offset) for i in range(size)])


def call(kernel, out_shape, **options):
    return pl.pallas_call(
        kernel,
        out_shape=out_shape,
        compiler_params=pltpu.CompilerParams(vmem_limit_bytes=VMEM_LIMIT),
        **options,
    )


def vmem():
    return pl.BlockSpec(memory_space=pltpu.VMEM)


def smem():
    return pl.BlockSpec(memory_space=pltpu.SMEM)


def flip(row, offset, chunk):
    width = row.shape[1]
    block = lax.broadcasted_iota(jnp.int32, row.shape, 1) // chunk
    bit = 0
    while offset >> bit:
        if (offset >> bit) & 1:
            stride = width // (2 * chunk) if bit == 0 else 1 << (bit - 1)
            ahead = pltpu.roll(row, width - stride * chunk, 1)
            back = pltpu.roll(row, stride * chunk, 1)
            row = jnp.where((block // stride) % 2 == 0, ahead, back)
        bit += 1
    return row


def in_local_order(blocks, me):
    ctx, tail = blocks.shape[0], blocks.shape[1:]
    stride = 1
    while stride < ctx:
        swapped = blocks.reshape((-1, 2, stride) + tail)[:, ::-1].reshape(blocks.shape)
        blocks = jnp.where((me // stride) % 2 == 1, swapped, blocks)
        stride *= 2
    return jnp.swapaxes(blocks.reshape((ctx // 2, 2) + tail), 0, 1).reshape(blocks.shape)


def logit_kernel(iq_a, iq_b, w_a, w_b, keys_t, out, rows):
    count = out.shape[0]
    depth = keys_t.shape[0]
    heads = iq_a.shape[1] // depth
    scale = depth ** -0.5
    weight = jnp.concatenate([w_a[...], w_b[...]], axis=0).astype(F32) * scale
    for j in range(heads):
        part = slice(j * depth, (j + 1) * depth)
        rows[j * count : (j + 1) * count, :] = jnp.concatenate([iq_a[:, part], iq_b[:, part]], axis=0)
    width = 256
    for first in range(0, keys_t.shape[1], width):
        cols = slice(first, first + width)
        score = matmul(rows[...], keys_t[:, cols])
        total = None
        for j in range(heads):
            term = weight[:, j : j + 1] * jnp.maximum(score[j * count : (j + 1) * count], 0.0)
            total = term if total is None else total + term
        out[:, cols] = total


def prob_kernel(scale, info, na, nb, ra, rb, up, keys_t, lse, pos, *rest):
    outs, row_sum, lhs, acc = rest[:-3], rest[-3], rest[-2], rest[-1]
    step = pl.program_id(0)
    group, depth, latent = up.shape
    count, keys = acc.shape
    rope = ra.shape[1] // group
    for i in range(group):
        part = slice(i * depth, (i + 1) * depth)
        query = jnp.concatenate([na[:, part], nb[:, part]], axis=0)
        lhs[i * count : (i + 1) * count, :latent] = matmul(query, up[i]).astype(BF16)
        low = (i * rope // LANES) * LANES
        pair = jnp.concatenate([ra[:, low : low + LANES], rb[:, low : low + LANES]], axis=0)
        shift = i * rope - low
        if shift:
            pair = jnp.concatenate([pair[:, shift:], pair[:, :shift]], axis=1)
        lhs[i * count : (i + 1) * count, latent:] = pair

    width = 256
    for first in range(0, keys, width):
        cols = slice(first, first + width)
        score = matmul(lhs[...], keys_t[:, cols])
        total = None
        for i in range(group):
            term = jnp.exp2(score[i * count : (i + 1) * count] * (scale * LOG2E) - lse[0, :, i : i + 1])
            total = term if total is None else total + term

        @pl.when(step == 0)
        def _():
            acc[:, cols] = total

        @pl.when(step > 0)
        def _():
            acc[:, cols] += total

    @pl.when(step == pl.num_programs(0) - 1)
    def _():
        key_pos = info[0] * keys + lax.broadcasted_iota(jnp.int32, (count, keys), 1)
        masked = jnp.where(key_pos <= pos[...], acc[...], 0.0)
        acc[...] = masked
        total = jnp.sum(masked, axis=1, keepdims=True)
        row_sum[...] = jnp.transpose(jnp.broadcast_to(total, (count, count)))[:8]
        size = count // len(outs)
        for k, out in enumerate(outs):
            start = pl.multiple_of(jnp.bitwise_xor(info[1], k) * size, size)
            out[...] = acc[pl.ds(start, size), :].astype(BF16)


def add_swapped_kernel(chunk, mine, other, out):
    out[...] = mine[...] + flip(other[...], 1, chunk)


def merge_kernel(chunk, peers, offsets, *refs):
    slices, totals, out = refs[:peers], refs[peers:-1], refs[-1]
    size = slices[0].shape[0]
    total = slices[0][...].astype(F32)
    for ref in slices[1:]:
        total = total + ref[...].astype(F32)
    out[:size, :] = total.astype(BF16)
    row = totals[0][...]
    for offset, ref in zip(offsets, totals[1:]):
        row = row + flip(ref[...], offset, chunk)
    row = jnp.concatenate([row, row], axis=0)
    width = row.shape[1]
    out[size:, :] = jnp.zeros((out.shape[0] - size, out.shape[1]), BF16)
    for i in range(3):
        piece = row.astype(BF16)
        out[size:, i * width : (i + 1) * width] = piece
        row = row - piece.astype(F32)


def grad_kernel(loss_scale, peers, info, *refs):
    slices = refs[:peers]
    logits, iq_a, iq_b, w_a, w_b, index_keys, keys_t, lse, pos = refs[peers : peers + 9]
    keep, away = refs[peers + 9 : peers + 11]
    dk_outs = refs[peers + 11 : 2 * peers + 11]
    rows, prob, dk = refs[2 * peers + 11 :]
    count, keys = logits.shape
    depth = keys_t.shape[0]
    heads = iq_a.shape[1] // depth
    half = count // 2
    scale = depth ** -0.5
    size = count // peers
    total = None
    for k, ref in enumerate(slices):
        start = pl.multiple_of(jnp.bitwise_xor(info[1], k) * size, size)
        prob[pl.ds(start, size), :] = ref[:size, :].astype(F32)
        for i in range(3):
            piece = ref[size : size + 16, i * count : (i + 1) * count].astype(F32)
            total = piece if total is None else total + piece
    square = (count, count)
    diagonal = lax.broadcasted_iota(jnp.int32, square, 0) == lax.broadcasted_iota(jnp.int32, square, 1)
    row_total = jnp.sum(
        jnp.where(diagonal, jnp.broadcast_to(total[:1], square), 0.0), axis=1, keepdims=True
    )
    key_pos = info[0] * keys + lax.broadcasted_iota(jnp.int32, (count, keys), 1)
    index_prob = jnp.where(key_pos <= pos[...], jnp.exp(logits[...] - lse[...]), 0.0)
    prob[...] = loss_scale * (index_prob - prob[...] / row_total)

    weight = jnp.concatenate([w_a[...], w_b[...]], axis=0).astype(F32)
    for j in range(heads):
        part = slice(j * depth, (j + 1) * depth)
        rows[j * count : (j + 1) * count, :] = jnp.concatenate([iq_a[:, part], iq_b[:, part]], axis=0)
    group = min(4, heads)
    for first in range(0, heads, group):
        mine = rows[first * count : (first + group) * count, :]
        score = matmul(mine, keys_t[...])
        d_score = jnp.concatenate(
            [
                jnp.where(
                    score[i * count : (i + 1) * count] > 0.0,
                    weight[:, first + i : first + i + 1] * prob[...],
                    0.0,
                ).astype(BF16)
                for i in range(group)
            ],
            axis=0,
        )
        dq = matmul(d_score, index_keys[...]) * scale
        for i in range(group):
            part = slice((first + i) * depth, (first + i + 1) * depth)
            keep[:, part] = dq[i * count : i * count + half]
            away[:, part] = dq[i * count + half : (i + 1) * count].astype(BF16)
        term = lax.dot_general(d_score, mine, (((0,), (0,)), ((), ())), preferred_element_type=F32)
        if first == 0:
            dk[...] = term
        else:
            dk[...] += term
    size = keys // peers
    for k, out in enumerate(dk_outs):
        start = pl.multiple_of(jnp.bitwise_xor(info[1], k) * size, size)
        out[...] = (dk[pl.ds(start, size), :] * scale).astype(out.dtype)


def fold_kernel(keep, other, own, *outs):
    chunk = own.shape[0]
    total = keep[...] + other[...].astype(F32)
    own[...] = total[:chunk]
    for i, out in enumerate(outs):
        out[...] = total[(i + 1) * chunk : (i + 2) * chunk].astype(BF16)


def final_kernel(chunks, *refs):
    parts, dk_parts, (dq_out, dk_out) = refs[:chunks], refs[chunks:-2], refs[-2:]
    total = parts[0][...]
    for ref in parts[1:]:
        total = total + ref[...].astype(F32)
    depth = dq_out.shape[2]
    for j in range(dq_out.shape[1]):
        dq_out[:, j, :] = total[:, j * depth : (j + 1) * depth]
    dk = dk_parts[0][...]
    for ref in dk_parts[1:]:
        dk = dk + ref[...].astype(F32)
    dk_out[...] = dk


def body(
    ctx,
    peers,
    query_heads,
    absorb_up,
    latent_keys,
    lse_heads,
    index_query,
    index_weight,
    index_keys,
    lse_index,
    query_pos,
    key_blocks,
):
    chunk, heads, width = query_heads.shape
    _, nope, latent = absorb_up.shape
    rope = width - nope
    keys = latent_keys.shape[0]
    index_heads, depth = index_query.shape[1:]
    count = chunk * ctx
    half = count // 2
    me = lax.axis_index("ctx")
    info = jnp.stack([key_blocks[0], lax.axis_index("head").astype(jnp.int32)])
    evens = list(range(2, ctx, 2))

    payload = jnp.concatenate(
        [
            query_heads[:, :, :nope].reshape(chunk, -1),
            query_heads[:, :, nope:].reshape(chunk, -1),
            index_query.reshape(chunk, -1),
            jnp.pad(index_weight, ((0, 0), (0, LANES - index_heads))),
        ],
        axis=1,
    )
    side_a = jnp.concatenate([payload] + [send(payload, "ctx", ctx, k) for k in evens], axis=0)
    side_b = send(side_a, "ctx", ctx, 1)

    local = jnp.concatenate(
        [lse_heads * LOG2E, lse_index[:, None], query_pos.astype(F32)[:, None]], axis=1
    )
    local = in_local_order(local.reshape(ctx, chunk, -1), me).reshape(count, -1)
    group = min(8, heads)
    steps = heads // group
    lse_groups = jnp.swapaxes(local[:, :heads].reshape(count, steps, group), 0, 1)
    lse_column = local[:, heads : heads + 1]
    pos_column = local[:, heads + 1 : heads + 2].astype(jnp.int32)

    latent_t = jnp.pad(latent_keys, ((0, 0), (0, LANES - rope))).T
    index_t = index_keys.T

    iq_width = index_heads * depth
    iq_spec = pl.BlockSpec((half, iq_width), lambda *_: (0, heads * width // iq_width))
    w_spec = pl.BlockSpec((half, LANES), lambda *_: (0, (heads * width + iq_width) // LANES))
    logit_part = call(
        logit_kernel,
        jax.ShapeDtypeStruct((count, keys), F32),
        grid=(1,),
        in_specs=[iq_spec, iq_spec, w_spec, w_spec, vmem()],
        out_specs=vmem(),
        scratch_shapes=[pltpu.VMEM((index_heads * count, depth), BF16)],
    )(side_a, side_b, side_a, side_b, index_t)
    logits = lax.psum(logit_part, "head")

    rope_first = heads * nope // (group * rope)
    nope_spec = pl.BlockSpec((half, group * nope), lambda g: (0, g))
    rope_spec = pl.BlockSpec((half, group * rope), lambda g: (0, rope_first + g))
    slice_shape = jax.ShapeDtypeStruct((count // peers, keys), BF16)
    *slices, row_sum = call(
        functools.partial(prob_kernel, width ** -0.5),
        [slice_shape] * peers + [jax.ShapeDtypeStruct((8, count), F32)],
        grid=(steps,),
        in_specs=[
            smem(),
            nope_spec,
            nope_spec,
            rope_spec,
            rope_spec,
            pl.BlockSpec((group, nope, latent), lambda g: (g, 0, 0)),
            vmem(),
            pl.BlockSpec((1, count, group), lambda g: (g, 0, 0)),
            vmem(),
        ],
        out_specs=[vmem()] * (peers + 1),
        scratch_shapes=[
            pltpu.VMEM((group * count, latent + LANES), BF16),
            pltpu.VMEM((count, keys), F32),
        ],
    )(info, side_a, side_b, side_a, side_b, absorb_up, latent_t, lse_groups, pos_column)

    row_sum = call(
        functools.partial(add_swapped_kernel, chunk),
        jax.ShapeDtypeStruct((8, count), F32),
    )(row_sum, send(row_sum, "ctx", ctx, 1))
    got = [slices[0]] + [send(slices[k], "head", peers, k) for k in range(1, peers)]
    totals = [row_sum] + [send(row_sum, "ctx", ctx, k) for k in evens]
    merged = call(
        functools.partial(merge_kernel, chunk, peers, evens),
        jax.ShapeDtypeStruct((count // peers + 16, keys), BF16),
    )(*got, *totals)
    gathered = [merged] + [send(merged, "head", peers, k) for k in range(1, peers)]

    loss_scale = (keys * ctx) ** 0.5
    dk_slice = (keys // peers, depth)
    outs = call(
        functools.partial(grad_kernel, loss_scale, peers),
        [
            jax.ShapeDtypeStruct((half, iq_width), F32),
            jax.ShapeDtypeStruct((half, iq_width), BF16),
            jax.ShapeDtypeStruct(dk_slice, F32),
        ]
        + [jax.ShapeDtypeStruct(dk_slice, BF16)] * (peers - 1),
        grid=(1,),
        in_specs=[smem()]
        + [vmem()] * peers
        + [vmem(), iq_spec, iq_spec, w_spec, w_spec, vmem(), vmem(), vmem(), vmem()],
        out_specs=[vmem()] * (peers + 2),
        scratch_shapes=[
            pltpu.VMEM((index_heads * count, depth), BF16),
            pltpu.VMEM((count, keys), F32),
            pltpu.VMEM((keys, depth), F32),
        ],
    )(
        info,
        *gathered,
        logits,
        side_a,
        side_b,
        side_a,
        side_b,
        index_keys,
        index_t,
        lse_column,
        pos_column,
    )
    keep, away, dk_own, *dk_away = outs
    other = send(away, "ctx", ctx, 1)
    dk_parts = [dk_own] + [send(dk_away[k - 1], "head", peers, k) for k in range(1, peers)]
    own, *parts = call(
        fold_kernel,
        [jax.ShapeDtypeStruct((chunk, iq_width), F32)]
        + [jax.ShapeDtypeStruct((chunk, iq_width), BF16)] * len(evens),
    )(keep, other)
    dq_parts = [own] + [send(part, "ctx", ctx, k) for part, k in zip(parts, evens)]
    return tuple(
        call(
            functools.partial(final_kernel, len(dq_parts)),
            [
                jax.ShapeDtypeStruct((chunk, index_heads, depth), F32),
                jax.ShapeDtypeStruct(dk_slice, F32),
            ],
        )(*dq_parts, *dk_parts)
    )


def solution(mesh):
    placed = (
        P("ctx", "head", None),
        P("head", None, None),
        P("ctx", None),
        P(None, "head"),
        P("ctx", "head", None),
        P("ctx", "head"),
        P("ctx", None),
        P(),
        P(),
        P("ctx"),
    )
    return jax.shard_map(
        functools.partial(body, mesh.shape["ctx"], mesh.shape["head"]),
        mesh=mesh,
        in_specs=placed,
        out_specs=(P("ctx", "head", None), P(("ctx", "head"), None)),
        check_vma=False,
    )
```

time: 207 us -> 106 us (0.51)
  waiting for transfers between devices: 105 us -> 25.3 us
  blocking collectives: 35.7 us -> 0 us
  matrix products: 30.2 us -> 0 us
  Pallas kernels: 0 us -> 27 us
  starting transfers between devices: 0.16 us -> 26.6 us
  other arithmetic: 11.1 us -> 1.36 us
    reduce_scatter x2 -> x0, waiting for transfers between devices: 53.9 us -> none  [the longest x1 31.1 us: body(): lax.psum_scatter(jnp.einsum('qjk,kd->qjd', d_score, index_keys, preferred...]
    psum x1, waiting for transfers between devices: 47.5 us -> 0.01 us  [body(): logits = lax.psum(logit_part, 'head')]
    dot_general x8 -> x0, matrix products: 30.2 us -> none  [the longest x4 16.5 us: add_group(): jnp.einsum('rgc,kc->rgk', query_group, latent_keys, preferred_element_typ...]
    pallas_call x0 -> x7, Pallas kernels: none -> 27 us  [the longest x1 19.1 us: body(): call(functools.partial(prob_kernel, width ** (-0.5)), [slice_shape] * pee...]
    ppermute x0 -> x21, starting transfers between devices: none -> 26.6 us  [send(): return lax.ppermute(array, axis, [(i, i ^ offset) for i in range(size)])]
    ppermute x0 -> x21, waiting for transfers between devices: none -> 25.3 us  [send(): return lax.ppermute(array, axis, [(i, i ^ offset) for i in range(size)])]
    all_gather x2 -> x0, blocking collectives: 21.9 us -> none  [the longest x1 11.2 us: body(): lax.all_gather(index_query, 'ctx', axis=0, tiled=True)]
    psum x1 -> x0, blocking collectives: 13.8 us -> none  [body(): row_total = lax.psum(jnp.sum(prob_sum, axis=1), 'ctx')]
  transfers between devices with their start and end apart: 4 -> 22, of which waited for: 4 -> 11; matrix products, arithmetic and copies ran while one was open for 7% -> 6% of each run, Pallas kernels for 0% -> 18%
where the time goes in v1:
time: 106 us; the launch traced here: 105 us
  Pallas kernels  27 us (25%)
  starting transfers between devices  26.6 us (25%)
  waiting for transfers between devices  25.3 us (24%)
  between operations  15 us (14%)
  local copies, waits for them, and re-layouts  10.1 us (10%)
  other arithmetic  1.36 us (1%)
    ppermute x21, starting transfers between devices, send(): return lax.ppermute(array, axis, [(i, i ^ offset) for i in range(size)])  26.6 us
    ppermute x21, waiting for transfers between devices, send(): return lax.ppermute(array, axis, [(i, i ^ offset) for i in range(size)])  25.3 us
    pallas_call x1, Pallas kernels, body(): call(functools.partial(prob_kernel, width ** (-0.5)), [slice_shape] * pee...  19.1 us
    pallas_call x1, Pallas kernels, body(): call(functools.partial(grad_kernel, loss_scale, peers), [jax.ShapeDtypeSt...  4.69 us
    concatenate x8, local copies, waits for them, and re-layouts, body(): jnp.concatenate([lse_heads * LOG2E, lse_index[:, None], query_pos.astype(...  3.56 us
    unnamed x12, local copies, waits for them, and re-layouts  2.22 us
    pallas_call x1, Pallas kernels, body(): call(logit_kernel, jax.ShapeDtypeStruct((count, keys), F32), grid=(1,), i...  2.16 us
  transfers between devices with their start and end apart: 22, of which 11 were waited for; matrix products, arithmetic and copies ran while one was open for 6% of the time, Pallas kernels for 18%

profile of v1, /device:TPU:0, one launch (start us, length us, event | category | flops | bytes accessed | tf_op | source)
XLA Modules:
  0.0 105.4 jit_solution(17617860855153908543)
XLA Ops:
  7.2 0.9 slice.15
  8.2 0.9 slice.16
  9.1 0.2 reshape.124
  9.3 0.9 copy.40
  10.2 0.7 pad.8
  10.9 3.0 %collective-permute-start = (bf16[16,8320]{1,0:T(8,128)(2,1)S(1)}, bf16[16,8320]{1,0:T(8,128)(2,1)S(1)}, u32[]{:S(2)}, u32[]{:S(2)}) collective-permute-start(bf16[16,8320]{1,0:T(8,128)(2,1)S(1)} %pad_maximum_fusion.1), channel_id=1, source_target_pairs={{0,8},{4,12},{8,0},{12,4},{16,24},{20,28},{24,16},{28,20},{1,9},{5... | collective-permute-start | bytes 798728 | tf_op jit(solution)/shard_map/ppermute | solution.py:23
  13.9 1.5 %collective-permute-start.1 = (bf16[16,8320]{1,0:T(8,128)(2,1)S(1)}, bf16[16,8320]{1,0:T(8,128)(2,1)S(1)}, u32[]{:S(2)}, u32[]{:S(2)}) collective-permute-start(bf16[16,8320]{1,0:T(8,128)(2,1)S(1)} %pad_maximum_fusion.1), channel_id=1, source_target_pairs={{0,16},{4,20},{8,24},{12,28},{16,0},{20,4},{24,8},{28,12},{1,17},{... | collective-permute-start | bytes 798728 | tf_op jit(solution)/shard_map/ppermute | solution.py:23
  15.4 0.7 convert_element_type.10
  16.1 0.2 concatenate.69
  16.3 0.2 concatenate.71
  16.5 0.9 concatenate.68
  17.4 0.9 concatenate.70
  18.2 0.2 concatenate.73
  18.4 0.9 concatenate.72
  19.3 0.2 concatenate.75
  19.5 0.2 concatenate.74
  19.9 1.2 %collective-permute-done = bf16[16,8320]{1,0:T(8,128)(2,1)S(1)} collective-permute-done((bf16[16,8320]{1,0:T(8,128)(2,1)S(1)}, bf16[16,8320]{1,0:T(8,128)(2,1)S(1)}, u32[]{:S(2)}, u32[]{:S(2)}) %collective-permute-start) | collective-permute-done | bytes 266272 | tf_op jit(solution)/shard_map/ppermute | solution.py:23
  21.1 6.3 %collective-permute-done.1 = bf16[16,8320]{1,0:T(8,128)(2,1)S(1)} collective-permute-done((bf16[16,8320]{1,0:T(8,128)(2,1)S(1)}, bf16[16,8320]{1,0:T(8,128)(2,1)S(1)}, u32[]{:S(2)}, u32[]{:S(2)}) %collective-permute-start.1) | collective-permute-done | bytes 266272 | tf_op jit(solution)/shard_map/ppermute | solution.py:23
  29.3 1.0 collective-permute-done.3.nb.rb.iq_b.w_b.refs_6_.refs_8_
  30.3 2.2 %shard_map.116 = f32[128,1024]{1,0:T(8,128)} custom-call(bf16[64,8320]{1,0:T(8,128)(2,1)S(1)} %pad_maximum_fusion.na.ra.iq_a.w_a.refs_5_.refs_7_, bf16[64,8320]{1,0:T(8,128)(2,1)S(1)} %collective-permute-done.3.nb.rb.iq_b.w_b.refs_6_.refs_8_, bf16[64,8320]{1,0:T(8,128)(2,1)S(1)} %pad_maximum_fusion.na.ra.iq_a.w_a.refs_5_.refs_7_, ...), custom_call_target="tpu_custom_call" | custom-call | tf_op jit(solution)/shard_map/pallas_call | solution.py:295
  32.5 1.4 %pad_bitcast_fusion.keys_t = bf16[640,1024]{1,0:T(8,128)(2,1)S(1)} fusion(bf16[1024,576]{0,1:T(8,128)(2,1)} %param.12), kind=kLoop, calls=%fused_computation | loop fusion | bytes 2490368 | tf_op jit(solution)/shard_map/transpose | solution.py:289
  34.0 19.1 %shard_map.113 = (bf16[32,1024]{1,0:T(8,128)(2,1)S(1)}, bf16[32,1024]{1,0:T(8,128)(2,1)S(1)}, bf16[32,1024]{1,0:T(8,128)(2,1)S(1)}, bf16[32,1024]{1,0:T(8,128)(2,1)S(1)}, f32[8,128]{1,0:T(8,128)S(1)}) custom-call(s32[2]{0:T(128)S(1)} %pad_add_fusion.info, bf16[64,8320]{1,0:T(8,128)(2,1)S(1)} %pad_maximum_fusion.na.ra.iq_a.w_a.refs_5_.refs_7_, ...), custom_call_target="tpu_custom_call" | custom-call | tf_op jit(solution)/shard_map/pallas_call | solution.py:309
  53.1 1.6 %collective-permute-start.4 = (bf16[32,1024]{1,0:T(8,128)(2,1)S(1)}, bf16[32,1024]{1,0:T(8,128)(2,1)S(1)}, u32[]{:S(2)}, u32[]{:S(2)}) collective-permute-start(bf16[32,1024]{1,0:T(8,128)(2,1)S(1)} %get-tuple-element.18), channel_id=1, source_target_pairs={{0,1},{1,0},{2,3},{3,2},{4,5},{5,4},{6,7},{7,6},{8,9},{9,8},{10,11... | collective-permute-start | bytes 196616 | tf_op jit(solution)/shard_map/ppermute | solution.py:23
  54.7 2.6 %collective-permute-start.5 = (bf16[32,1024]{1,0:T(8,128)(2,1)S(1)}, bf16[32,1024]{1,0:T(8,128)(2,1)S(1)}, u32[]{:S(2)}, u32[]{:S(2)}) collective-permute-start(bf16[32,1024]{1,0:T(8,128)(2,1)S(1)} %get-tuple-element.19), channel_id=1, source_target_pairs={{0,2},{1,3},{2,0},{3,1},{4,6},{5,7},{6,4},{7,5},{8,10},{9,11},{10,... | collective-permute-start | bytes 196616 | tf_op jit(solution)/shard_map/ppermute | solution.py:23
  57.3 0.2 collective-permute-start.6
  57.5 1.2 %collective-permute-done.7.other = f32[8,128]{1,0:T(8,128)S(1)} collective-permute-done((f32[8,128]{1,0:T(8,128)S(1)}, f32[8,128]{1,0:T(8,128)S(1)}, u32[]{:S(2)}, u32[]{:S(2)}) %collective-permute-start.7) | collective-permute-done | bytes 4128 | tf_op jit(solution)/shard_map/ppermute | solution.py:23
  58.8 1.5 %collective-permute-start.10 = (f32[8,128]{1,0:T(8,128)S(1)}, f32[8,128]{1,0:T(8,128)S(1)}, u32[]{:S(2)}, u32[]{:S(2)}) collective-permute-start(f32[8,128]{1,0:T(8,128)S(1)} %shard_map.114.refs_4_), channel_id=1, source_target_pairs={{0,24},{4,28},{8,16},{12,20},{16,8},{20,12},{24,0},{28,4},{1,25},{... | collective-permute-start | bytes 12296 | tf_op jit(solution)/shard_map/ppermute | solution.py:23
  60.2 1.5 %collective-permute-start.8 = (f32[8,128]{1,0:T(8,128)S(1)}, f32[8,128]{1,0:T(8,128)S(1)}, u32[]{:S(2)}, u32[]{:S(2)}) collective-permute-start(f32[8,128]{1,0:T(8,128)S(1)} %shard_map.114.refs_4_), channel_id=1, source_target_pairs={{0,8},{4,12},{8,0},{12,4},{16,24},{20,28},{24,16},{28,20},{1,9},{5... | collective-permute-start | bytes 12296 | tf_op jit(solution)/shard_map/ppermute | solution.py:23
  61.7 1.5 %collective-permute-done.10.refs_7_ = f32[8,128]{1,0:T(8,128)S(1)} collective-permute-done((f32[8,128]{1,0:T(8,128)S(1)}, f32[8,128]{1,0:T(8,128)S(1)}, u32[]{:S(2)}, u32[]{:S(2)}) %collective-permute-start.10) | collective-permute-done | bytes 4128 | tf_op jit(solution)/shard_map/ppermute | solution.py:23
  63.3 1.5 %collective-permute-start.9 = (f32[8,128]{1,0:T(8,128)S(1)}, f32[8,128]{1,0:T(8,128)S(1)}, u32[]{:S(2)}, u32[]{:S(2)}) collective-permute-start(f32[8,128]{1,0:T(8,128)S(1)} %shard_map.114.refs_4_), channel_id=1, source_target_pairs={{0,16},{4,20},{8,24},{12,28},{16,0},{20,4},{24,8},{28,12},{1,17},{... | collective-permute-start | bytes 12296 | tf_op jit(solution)/shard_map/ppermute | solution.py:23
  64.8 2.1 %collective-permute-done.9.refs_6_ = f32[8,128]{1,0:T(8,128)S(1)} collective-permute-done((f32[8,128]{1,0:T(8,128)S(1)}, f32[8,128]{1,0:T(8,128)S(1)}, u32[]{:S(2)}, u32[]{:S(2)}) %collective-permute-start.9) | collective-permute-done | bytes 4128 | tf_op jit(solution)/shard_map/ppermute | solution.py:23
  67.0 1.0 collective-permute-start.11
  68.1 3.1 %collective-permute-start.12 = (bf16[48,1024]{1,0:T(8,128)(2,1)S(1)}, bf16[48,1024]{1,0:T(8,128)(2,1)S(1)}, u32[]{:S(2)}, u32[]{:S(2)}) collective-permute-start(bf16[48,1024]{1,0:T(8,128)(2,1)S(1)} %shard_map.115.refs_0_), channel_id=1, source_target_pairs={{0,2},{1,3},{2,0},{3,1},{4,6},{5,7},{6,4},{7,5},{8,10},{9,11},{10,... | collective-permute-start | bytes 294920 | tf_op jit(solution)/shard_map/ppermute | solution.py:23
  71.2 0.8 collective-permute-start.13
  72.0 2.8 %collective-permute-done.11.refs_1_ = bf16[48,1024]{1,0:T(8,128)(2,1)S(1)} collective-permute-done((bf16[48,1024]{1,0:T(8,128)(2,1)S(1)}, bf16[48,1024]{1,0:T(8,128)(2,1)S(1)}, u32[]{:S(2)}, u32[]{:S(2)}) %collective-permute-start.11) | collective-permute-done | bytes 98336 | tf_op jit(solution)/shard_map/ppermute | solution.py:23
  74.8 5.6 %collective-permute-done.12.refs_2_ = bf16[48,1024]{1,0:T(8,128)(2,1)S(1)} collective-permute-done((bf16[48,1024]{1,0:T(8,128)(2,1)S(1)}, bf16[48,1024]{1,0:T(8,128)(2,1)S(1)}, u32[]{:S(2)}, u32[]{:S(2)}) %collective-permute-start.12) | collective-permute-done | bytes 98336 | tf_op jit(solution)/shard_map/ppermute | solution.py:23
  80.4 1.0 copy-done.1
  81.5 4.7 %shard_map.117 = (f32[64,2048]{1,0:T(8,128)S(1)}, bf16[64,2048]{1,0:T(8,128)(2,1)S(1)}, f32[256,128]{1,0:T(8,128)S(1)}, bf16[256,128]{1,0:T(8,128)(2,1)S(1)}, bf...) custom-call(s32[2]{0:T(128)S(1)} %pad_add_fusion.info, bf16[48,1024]{1,0:T(8,128)(2,1)S(1)} %shard_map.115.refs_0_, ...), custom_call_target="tpu_custom_call" | custom-call | tf_op jit(solution)/shard_map/pallas_call | solution.py:345
  86.2 1.7 %collective-permute-start.18 = (bf16[256,128]{1,0:T(8,128)(2,1)S(1)}, bf16[256,128]{1,0:T(8,128)(2,1)S(1)}, u32[]{:S(2)}, u32[]{:S(2)}) collective-permute-start(bf16[256,128]{1,0:T(8,128)(2,1)S(1)} %get-tuple-element.29), channel_id=1, source_target_pairs={{0,1},{1,0},{2,3},{3,2},{4,5},{5,4},{6,7},{7,6},{8,9},{9,8},{10,11... | collective-permute-start | bytes 196616 | tf_op jit(solution)/shard_map/ppermute | solution.py:23
  87.9 1.0 collective-permute-start.19
  88.9 1.8 %collective-permute-start.20 = (bf16[256,128]{1,0:T(8,128)(2,1)S(1)}, bf16[256,128]{1,0:T(8,128)(2,1)S(1)}, u32[]{:S(2)}, u32[]{:S(2)}) collective-permute-start(bf16[256,128]{1,0:T(8,128)(2,1)S(1)} %get-tuple-element.31), channel_id=1, source_target_pairs={{0,3},{1,2},{2,1},{3,0},{4,7},{5,6},{6,5},{7,4},{8,11},{9,10},{10,... | collective-permute-start | bytes 196616 | tf_op jit(solution)/shard_map/ppermute | solution.py:23
  90.7 1.1 %collective-permute-start.15 = (bf16[16,2048]{1,0:T(8,128)(2,1)S(1)}, bf16[16,2048]{1,0:T(8,128)(2,1)S(1)}, u32[]{:S(2)}, u32[]{:S(2)}) collective-permute-start(bf16[16,2048]{1,0:T(8,128)(2,1)S(1)} %get-tuple-element.25), channel_id=1, source_target_pairs={{0,8},{4,12},{8,0},{12,4},{16,24},{20,28},{24,16},{28,20},{1,9},{5... | collective-permute-start | bytes 196616 | tf_op jit(solution)/shard_map/ppermute | solution.py:23
  91.8 0.8 collective-permute-start.16
  92.6 1.7 %collective-permute-start.17 = (bf16[16,2048]{1,0:T(8,128)(2,1)S(1)}, bf16[16,2048]{1,0:T(8,128)(2,1)S(1)}, u32[]{:S(2)}, u32[]{:S(2)}) collective-permute-start(bf16[16,2048]{1,0:T(8,128)(2,1)S(1)} %get-tuple-element.27), channel_id=1, source_target_pairs={{0,24},{4,28},{8,16},{12,20},{16,8},{20,12},{24,0},{28,4},{1,25},{... | collective-permute-start | bytes 196616 | tf_op jit(solution)/shard_map/ppermute | solution.py:23
  94.3 2.1 %collective-permute-done.19.refs_6_ = bf16[256,128]{1,0:T(8,128)(2,1)S(1)} collective-permute-done((bf16[256,128]{1,0:T(8,128)(2,1)S(1)}, bf16[256,128]{1,0:T(8,128)(2,1)S(1)}, u32[]{:S(2)}, u32[]{:S(2)}) %collective-permute-start.19) | collective-permute-done | bytes 65568 | tf_op jit(solution)/shard_map/ppermute | solution.py:23
  96.4 0.4 collective-permute-done.16.refs_2_
  96.8 1.0 collective-permute-done.17.refs_3_
  97.8 0.8 shard_map.119
  (45 shorter events, 1.8 us)
Async XLA Ops:
  7.2 12.4 %copy-start.3 = (f32[128]{0:T(128)S(1)}, f32[128]{0:T(128)}, u32[]{:S(2)}) copy-start(f32[128]{0:T(128)} %param.17) | copy-start | bytes 1540
  7.2 12.6 %copy-start.2 = (f32[128,32]{0,1:T(8,128)S(1)}, f32[128,32]{0,1:T(8,128)}, u32[]{:S(2)}) copy-start(f32[128,32]{0,1:T(8,128)} %param.13) | copy-start | bytes 49156
  7.2 73.2 %all-reduce.4.cloned.1.call-start = ((), (), s32[]{:S(2)}) async-start(), calls=%async_computation | async-start | bytes 1048576 | tf_op jit(solution)/shard_map/psum | solution.py:303
  10.9 10.2 %collective-permute-start = (bf16[16,8320]{1,0:T(8,128)(2,1)S(1)}, bf16[16,8320]{1,0:T(8,128)(2,1)S(1)}, u32[]{:S(2)}, u32[]{:S(2)}) collective-permute-start(bf16[16,8320]{1,0:T(8,128)(2,1)S(1)} %pad_maximum_fusion.1), channel_id=1, source_target_pairs={{0,8},{4,12},{8,0},{12,4},{16,24},{20,28},{24,16},{28,20},{1,9},{5... | collective-permute-start | bytes 798728 | tf_op jit(solution)/shard_map/ppermute | solution.py:23
  13.9 13.6 %collective-permute-start.1 = (bf16[16,8320]{1,0:T(8,128)(2,1)S(1)}, bf16[16,8320]{1,0:T(8,128)(2,1)S(1)}, u32[]{:S(2)}, u32[]{:S(2)}) collective-permute-start(bf16[16,8320]{1,0:T(8,128)(2,1)S(1)} %pad_maximum_fusion.1), channel_id=1, source_target_pairs={{0,16},{4,20},{8,24},{12,28},{16,0},{20,4},{24,8},{28,12},{1,17},{... | collective-permute-start | bytes 798728 | tf_op jit(solution)/shard_map/ppermute | solution.py:23
  15.4 12.0 %collective-permute-start.2 = (bf16[16,8320]{1,0:T(8,128)(2,1)S(1)}, bf16[16,8320]{1,0:T(8,128)(2,1)S(1)}, u32[]{:S(2)}, u32[]{:S(2)}) collective-permute-start(bf16[16,8320]{1,0:T(8,128)(2,1)S(1)} %pad_maximum_fusion.1), channel_id=1, source_target_pairs={{0,24},{4,28},{8,16},{12,20},{16,8},{20,12},{24,0},{28,4},{1,25},{... | collective-permute-start | bytes 798728 | tf_op jit(solution)/shard_map/ppermute | solution.py:23
  19.9 9.1 %copy-start = (bf16[1024,128]{1,0:T(8,128)(2,1)S(1)}, bf16[1024,128]{1,0:T(8,128)(2,1)}, u32[]{:S(2)}) copy-start(bf16[1024,128]{1,0:T(8,128)(2,1)} %refs_9_.1) | copy-start | bytes 786436
  27.6 2.7 %collective-permute-start.3 = (bf16[64,8320]{1,0:T(8,128)(2,1)S(1)}, bf16[64,8320]{1,0:T(8,128)(2,1)S(1)}, u32[]{:S(2)}, u32[]{:S(2)}) collective-permute-start(bf16[64,8320]{1,0:T(8,128)(2,1)S(1)} %pad_maximum_fusion.na.ra.iq_a.w_a.refs_5_.refs_7_), channel_id=1, source_target_pairs={{0,4},{4,0},{8,12},{12,8},{16,20},{20,16},{24,28},{28,24},{1,5},{5... | collective-permute-start | bytes 3194888 | tf_op jit(solution)/shard_map/ppermute | solution.py:23
  53.1 13.8 %collective-permute-start.4 = (bf16[32,1024]{1,0:T(8,128)(2,1)S(1)}, bf16[32,1024]{1,0:T(8,128)(2,1)S(1)}, u32[]{:S(2)}, u32[]{:S(2)}) collective-permute-start(bf16[32,1024]{1,0:T(8,128)(2,1)S(1)} %get-tuple-element.18), channel_id=1, source_target_pairs={{0,1},{1,0},{2,3},{3,2},{4,5},{5,4},{6,7},{7,6},{8,9},{9,8},{10,11... | collective-permute-start | bytes 196616 | tf_op jit(solution)/shard_map/ppermute | solution.py:23
  54.7 12.2 %collective-permute-start.5 = (bf16[32,1024]{1,0:T(8,128)(2,1)S(1)}, bf16[32,1024]{1,0:T(8,128)(2,1)S(1)}, u32[]{:S(2)}, u32[]{:S(2)}) collective-permute-start(bf16[32,1024]{1,0:T(8,128)(2,1)S(1)} %get-tuple-element.19), channel_id=1, source_target_pairs={{0,2},{1,3},{2,0},{3,1},{4,6},{5,7},{6,4},{7,5},{8,10},{9,11},{10,... | collective-permute-start | bytes 196616 | tf_op jit(solution)/shard_map/ppermute | solution.py:23
  57.3 9.6 %collective-permute-start.6 = (bf16[32,1024]{1,0:T(8,128)(2,1)S(1)}, bf16[32,1024]{1,0:T(8,128)(2,1)S(1)}, u32[]{:S(2)}, u32[]{:S(2)}) collective-permute-start(bf16[32,1024]{1,0:T(8,128)(2,1)S(1)} %get-tuple-element.20), channel_id=1, source_target_pairs={{0,3},{1,2},{2,1},{3,0},{4,7},{5,6},{6,5},{7,4},{8,11},{9,10},{10,... | collective-permute-start | bytes 196616 | tf_op jit(solution)/shard_map/ppermute | solution.py:23
  57.5 1.2 %collective-permute-start.7 = (f32[8,128]{1,0:T(8,128)S(1)}, f32[8,128]{1,0:T(8,128)S(1)}, u32[]{:S(2)}, u32[]{:S(2)}) collective-permute-start(f32[8,128]{1,0:T(8,128)S(1)} %get-tuple-element.21.mine), channel_id=1, source_target_pairs={{0,4},{4,0},{8,12},{12,8},{16,20},{20,16},{24,28},{28,24},{1,5},{5... | collective-permute-start | bytes 12296 | tf_op jit(solution)/shard_map/ppermute | solution.py:23
  58.8 4.5 %collective-permute-start.10 = (f32[8,128]{1,0:T(8,128)S(1)}, f32[8,128]{1,0:T(8,128)S(1)}, u32[]{:S(2)}, u32[]{:S(2)}) collective-permute-start(f32[8,128]{1,0:T(8,128)S(1)} %shard_map.114.refs_4_), channel_id=1, source_target_pairs={{0,24},{4,28},{8,16},{12,20},{16,8},{20,12},{24,0},{28,4},{1,25},{... | collective-permute-start | bytes 12296 | tf_op jit(solution)/shard_map/ppermute | solution.py:23
  60.2 4.5 %collective-permute-start.8 = (f32[8,128]{1,0:T(8,128)S(1)}, f32[8,128]{1,0:T(8,128)S(1)}, u32[]{:S(2)}, u32[]{:S(2)}) collective-permute-start(f32[8,128]{1,0:T(8,128)S(1)} %shard_map.114.refs_4_), channel_id=1, source_target_pairs={{0,8},{4,12},{8,0},{12,4},{16,24},{20,28},{24,16},{28,20},{1,9},{5... | collective-permute-start | bytes 12296 | tf_op jit(solution)/shard_map/ppermute | solution.py:23
  63.3 3.6 %collective-permute-start.9 = (f32[8,128]{1,0:T(8,128)S(1)}, f32[8,128]{1,0:T(8,128)S(1)}, u32[]{:S(2)}, u32[]{:S(2)}) collective-permute-start(f32[8,128]{1,0:T(8,128)S(1)} %shard_map.114.refs_4_), channel_id=1, source_target_pairs={{0,16},{4,20},{8,24},{12,28},{16,0},{20,4},{24,8},{28,12},{1,17},{... | collective-permute-start | bytes 12296 | tf_op jit(solution)/shard_map/ppermute | solution.py:23
  67.0 7.8 %collective-permute-start.11 = (bf16[48,1024]{1,0:T(8,128)(2,1)S(1)}, bf16[48,1024]{1,0:T(8,128)(2,1)S(1)}, u32[]{:S(2)}, u32[]{:S(2)}) collective-permute-start(bf16[48,1024]{1,0:T(8,128)(2,1)S(1)} %shard_map.115.refs_0_), channel_id=1, source_target_pairs={{0,1},{1,0},{2,3},{3,2},{4,5},{5,4},{6,7},{7,6},{8,9},{9,8},{10,11... | collective-permute-start | bytes 294920 | tf_op jit(solution)/shard_map/ppermute | solution.py:23
  68.1 12.3 %collective-permute-start.12 = (bf16[48,1024]{1,0:T(8,128)(2,1)S(1)}, bf16[48,1024]{1,0:T(8,128)(2,1)S(1)}, u32[]{:S(2)}, u32[]{:S(2)}) collective-permute-start(bf16[48,1024]{1,0:T(8,128)(2,1)S(1)} %shard_map.115.refs_0_), channel_id=1, source_target_pairs={{0,2},{1,3},{2,0},{3,1},{4,6},{5,7},{6,4},{7,5},{8,10},{9,11},{10,... | collective-permute-start | bytes 294920 | tf_op jit(solution)/shard_map/ppermute | solution.py:23
  71.2 9.2 %collective-permute-start.13 = (bf16[48,1024]{1,0:T(8,128)(2,1)S(1)}, bf16[48,1024]{1,0:T(8,128)(2,1)S(1)}, u32[]{:S(2)}, u32[]{:S(2)}) collective-permute-start(bf16[48,1024]{1,0:T(8,128)(2,1)S(1)} %shard_map.115.refs_0_), channel_id=1, source_target_pairs={{0,3},{1,2},{2,1},{3,0},{4,7},{5,6},{6,5},{7,4},{8,11},{9,10},{10,... | collective-permute-start | bytes 294920 | tf_op jit(solution)/shard_map/ppermute | solution.py:23
  80.4 1.0 copy-start.1
  86.1 4.5 %collective-permute-start.14 = (bf16[64,2048]{1,0:T(8,128)(2,1)S(1)}, bf16[64,2048]{1,0:T(8,128)(2,1)S(1)}, u32[]{:S(2)}, u32[]{:S(2)}) collective-permute-start(bf16[64,2048]{1,0:T(8,128)(2,1)S(1)} %get-tuple-element.23), channel_id=1, source_target_pairs={{0,4},{4,0},{8,12},{12,8},{16,20},{20,16},{24,28},{28,24},{1,5},{5... | collective-permute-start | bytes 786440 | tf_op jit(solution)/shard_map/ppermute | solution.py:23
  86.2 6.4 %collective-permute-start.18 = (bf16[256,128]{1,0:T(8,128)(2,1)S(1)}, bf16[256,128]{1,0:T(8,128)(2,1)S(1)}, u32[]{:S(2)}, u32[]{:S(2)}) collective-permute-start(bf16[256,128]{1,0:T(8,128)(2,1)S(1)} %get-tuple-element.29), channel_id=1, source_target_pairs={{0,1},{1,0},{2,3},{3,2},{4,5},{5,4},{6,7},{7,6},{8,9},{9,8},{10,11... | collective-permute-start | bytes 196616 | tf_op jit(solution)/shard_map/ppermute | solution.py:23
  87.9 8.4 %collective-permute-start.19 = (bf16[256,128]{1,0:T(8,128)(2,1)S(1)}, bf16[256,128]{1,0:T(8,128)(2,1)S(1)}, u32[]{:S(2)}, u32[]{:S(2)}) collective-permute-start(bf16[256,128]{1,0:T(8,128)(2,1)S(1)} %get-tuple-element.30), channel_id=1, source_target_pairs={{0,2},{1,3},{2,0},{3,1},{4,6},{5,7},{6,4},{7,5},{8,10},{9,11},{10,... | collective-permute-start | bytes 196616 | tf_op jit(solution)/shard_map/ppermute | solution.py:23
  88.9 7.4 %collective-permute-start.20 = (bf16[256,128]{1,0:T(8,128)(2,1)S(1)}, bf16[256,128]{1,0:T(8,128)(2,1)S(1)}, u32[]{:S(2)}, u32[]{:S(2)}) collective-permute-start(bf16[256,128]{1,0:T(8,128)(2,1)S(1)} %get-tuple-element.31), channel_id=1, source_target_pairs={{0,3},{1,2},{2,1},{3,0},{4,7},{5,6},{6,5},{7,4},{8,11},{9,10},{10,... | collective-permute-start | bytes 196616 | tf_op jit(solution)/shard_map/ppermute | solution.py:23
  90.7 5.6 %collective-permute-start.15 = (bf16[16,2048]{1,0:T(8,128)(2,1)S(1)}, bf16[16,2048]{1,0:T(8,128)(2,1)S(1)}, u32[]{:S(2)}, u32[]{:S(2)}) collective-permute-start(bf16[16,2048]{1,0:T(8,128)(2,1)S(1)} %get-tuple-element.25), channel_id=1, source_target_pairs={{0,8},{4,12},{8,0},{12,4},{16,24},{20,28},{24,16},{28,20},{1,9},{5... | collective-permute-start | bytes 196616 | tf_op jit(solution)/shard_map/ppermute | solution.py:23
  91.8 5.0 %collective-permute-start.16 = (bf16[16,2048]{1,0:T(8,128)(2,1)S(1)}, bf16[16,2048]{1,0:T(8,128)(2,1)S(1)}, u32[]{:S(2)}, u32[]{:S(2)}) collective-permute-start(bf16[16,2048]{1,0:T(8,128)(2,1)S(1)} %get-tuple-element.26), channel_id=1, source_target_pairs={{0,16},{4,20},{8,24},{12,28},{16,0},{20,4},{24,8},{28,12},{1,17},{... | collective-permute-start | bytes 196616 | tf_op jit(solution)/shard_map/ppermute | solution.py:23
  92.6 5.2 %collective-permute-start.17 = (bf16[16,2048]{1,0:T(8,128)(2,1)S(1)}, bf16[16,2048]{1,0:T(8,128)(2,1)S(1)}, u32[]{:S(2)}, u32[]{:S(2)}) collective-permute-start(bf16[16,2048]{1,0:T(8,128)(2,1)S(1)} %get-tuple-element.27), channel_id=1, source_target_pairs={{0,24},{4,28},{8,16},{12,20},{16,8},{20,12},{24,0},{28,4},{1,25},{... | collective-permute-start | bytes 196616 | tf_op jit(solution)/shard_map/ppermute | solution.py:23
Sparse Core Ops, SparseCore 0:
  32.6 43.0 all-reduce.3

commit v2 on v1

--- a/solution.py
+++ b/solution.py
@@ -21,6 +21,10 @@
 
 def send(array, axis, size, offset):
     return lax.ppermute(array, axis, [(i, i ^ offset) for i in range(size)])
+
+
+def swap_heads(slices, peers):
+    return [slices[0]] + [send(slices[k], "head", peers, k) for k in range(1, peers)]
 
 
 def call(kernel, out_shape, **options):
@@ -64,8 +68,9 @@
     return jnp.swapaxes(blocks.reshape((ctx // 2, 2) + tail), 0, 1).reshape(blocks.shape)
 
 
-def logit_kernel(iq_a, iq_b, w_a, w_b, keys_t, out, rows):
-    count = out.shape[0]
+def logit_kernel(info, iq_a, iq_b, w_a, w_b, keys_t, *rest):
+    outs, rows, acc = rest[:-2], rest[-2], rest[-1]
+    count = acc.shape[0]
     depth = keys_t.shape[0]
     heads = iq_a.shape[1] // depth
     scale = depth ** -0.5
@@ -73,19 +78,26 @@
     for j in range(heads):
         part = slice(j * depth, (j + 1) * depth)
         rows[j * count : (j + 1) * count, :] = jnp.concatenate([iq_a[:, part], iq_b[:, part]], axis=0)
-    width = 256
-    for first in range(0, keys_t.shape[1], width):
-        cols = slice(first, first + width)
-        score = matmul(rows[...], keys_t[:, cols])
+    group = min(4, heads)
+    for first in range(0, heads, group):
+        score = matmul(rows[first * count : (first + group) * count, :], keys_t[...])
         total = None
-        for j in range(heads):
-            term = weight[:, j : j + 1] * jnp.maximum(score[j * count : (j + 1) * count], 0.0)
+        for i in range(group):
+            j = first + i
+            term = weight[:, j : j + 1] * jnp.maximum(score[i * count : (i + 1) * count], 0.0)
             total = term if total is None else total + term
-        out[:, cols] = total
+        if first == 0:
+            acc[...] = total
+        else:
+            acc[...] += total
+    size = count // len(outs)
+    for k, out in enumerate(outs):
+        start = pl.multiple_of(jnp.bitwise_xor(info[1], k) * size, size)
+        out[...] = acc[pl.ds(start, size), :]
 
 
 def prob_kernel(scale, info, na, nb, ra, rb, up, keys_t, lse, pos, *rest):
-    outs, row_sum, lhs, acc = rest[:-3], rest[-3], rest[-2], rest[-1]
+    outs, lhs, acc = rest[:-2], rest[-2], rest[-1]
     step = pl.program_id(0)
     group, depth, latent = up.shape
     count, keys = acc.shape
@@ -101,22 +113,19 @@
             pair = jnp.concatenate([pair[:, shift:], pair[:, :shift]], axis=1)
         lhs[i * count : (i + 1) * count, latent:] = pair
 
-    width = 256
-    for first in range(0, keys, width):
-        cols = slice(first, first + width)
-        score = matmul(lhs[...], keys_t[:, cols])
-        total = None
-        for i in range(group):
-            term = jnp.exp2(score[i * count : (i + 1) * count] * (scale * LOG2E) - lse[0, :, i : i + 1])
-            total = term if total is None else total + term
-
-        @pl.when(step == 0)
-        def _():
-            acc[:, cols] = total
-
-        @pl.when(step > 0)
-        def _():
-            acc[:, cols] += total
+    score = matmul(lhs[...], keys_t[...])
+    total = None
+    for i in range(group):
+        term = jnp.exp2(score[i * count : (i + 1) * count] * (scale * LOG2E) - lse[0, :, i : i + 1])
+        total = term if total is None else total + term
+
+    @pl.when(step == 0)
+    def _():
+        acc[...] = total
+
+    @pl.when(step > 0)
+    def _():
+        acc[...] += total
 
     @pl.when(step == pl.num_programs(0) - 1)
     def _():
@@ -124,63 +133,69 @@
         masked = jnp.where(key_pos <= pos[...], acc[...], 0.0)
         acc[...] = masked
         total = jnp.sum(masked, axis=1, keepdims=True)
-        row_sum[...] = jnp.transpose(jnp.broadcast_to(total, (count, count)))[:8]
         size = count // len(outs)
+        row = jnp.transpose(jnp.broadcast_to(total, (count, count)))[:size]
+        line = lax.broadcasted_iota(jnp.int32, row.shape, 0)
+        high = row.astype(BF16).astype(F32)
+        middle = (row - high).astype(BF16).astype(F32)
+        low = row - high - middle
+        packed = jnp.where(line == 0, high, jnp.where(line == 1, middle, jnp.where(line == 2, low, 0.0)))
         for k, out in enumerate(outs):
             start = pl.multiple_of(jnp.bitwise_xor(info[1], k) * size, size)
-            out[...] = acc[pl.ds(start, size), :].astype(BF16)
+            out[:, :keys] = acc[pl.ds(start, size), :].astype(BF16)
+            out[:, keys:] = packed.astype(BF16)
 
 
 def add_swapped_kernel(chunk, mine, other, out):
     out[...] = mine[...] + flip(other[...], 1, chunk)
 
 
-def merge_kernel(chunk, peers, offsets, *refs):
-    slices, totals, out = refs[:peers], refs[peers:-1], refs[-1]
-    size = slices[0].shape[0]
-    total = slices[0][...].astype(F32)
+def merge_kernel(*refs):
+    slices, out, row_sum = refs[:-2], refs[-2], refs[-1]
+    keys = out.shape[1]
+    total = None
+    for ref in slices:
+        part = ref[...].astype(F32)
+        total = part if total is None else total + part
+    out[...] = total[:, :keys].astype(BF16)
+    row = jnp.sum(total[:, keys:], axis=0, keepdims=True)
+    row_sum[...] = jnp.broadcast_to(row, row_sum.shape)
+
+
+def index_prob_kernel(info, lse, pos, *refs):
+    slices, out = refs[:-1], refs[-1]
+    size, keys = out.shape
+    total = slices[0][...]
     for ref in slices[1:]:
-        total = total + ref[...].astype(F32)
-    out[:size, :] = total.astype(BF16)
-    row = totals[0][...]
-    for offset, ref in zip(offsets, totals[1:]):
-        row = row + flip(ref[...], offset, chunk)
-    row = jnp.concatenate([row, row], axis=0)
-    width = row.shape[1]
-    out[size:, :] = jnp.zeros((out.shape[0] - size, out.shape[1]), BF16)
-    for i in range(3):
-        piece = row.astype(BF16)
-        out[size:, i * width : (i + 1) * width] = piece
-        row = row - piece.astype(F32)
-
-
-def grad_kernel(loss_scale, peers, info, *refs):
-    slices = refs[:peers]
-    logits, iq_a, iq_b, w_a, w_b, index_keys, keys_t, lse, pos = refs[peers : peers + 9]
-    keep, away = refs[peers + 9 : peers + 11]
-    dk_outs = refs[peers + 11 : 2 * peers + 11]
-    rows, prob, dk = refs[2 * peers + 11 :]
-    count, keys = logits.shape
+        total = total + ref[...]
+    rows = pl.ds(pl.multiple_of(info[1] * size, size), size)
+    key_pos = info[0] * keys + lax.broadcasted_iota(jnp.int32, (size, keys), 1)
+    out[...] = jnp.where(key_pos <= pos[rows, :], jnp.exp(total - lse[rows, :]), 0.0).astype(BF16)
+
+
+def grad_kernel(loss_scale, chunk, peers, offsets, info, *refs):
+    slices, refs = refs[:peers], refs[peers:]
+    index_slices, refs = refs[:peers], refs[peers:]
+    totals, refs = refs[: len(offsets) + 1], refs[len(offsets) + 1 :]
+    iq_a, iq_b, w_a, w_b, index_keys, keys_t, keep, away = refs[:8]
+    dk_outs, (rows, prob, dk) = refs[8:-3], refs[-3:]
+    count, keys = prob.shape
     depth = keys_t.shape[0]
     heads = iq_a.shape[1] // depth
     half = count // 2
     scale = depth ** -0.5
     size = count // peers
-    total = None
-    for k, ref in enumerate(slices):
-        start = pl.multiple_of(jnp.bitwise_xor(info[1], k) * size, size)
-        prob[pl.ds(start, size), :] = ref[:size, :].astype(F32)
-        for i in range(3):
-            piece = ref[size : size + 16, i * count : (i + 1) * count].astype(F32)
-            total = piece if total is None else total + piece
+    row = totals[0][...]
+    for offset, ref in zip(offsets, totals[1:]):
+        row = row + flip(ref[...], offset, chunk)
     square = (count, count)
     diagonal = lax.broadcasted_iota(jnp.int32, square, 0) == lax.broadcasted_iota(jnp.int32, square, 1)
-    row_total = jnp.sum(
-        jnp.where(diagonal, jnp.broadcast_to(total[:1], square), 0.0), axis=1, keepdims=True
-    )
-    key_pos = info[0] * keys + lax.broadcasted_iota(jnp.int32, (count, keys), 1)
-    index_prob = jnp.where(key_pos <= pos[...], jnp.exp(logits[...] - lse[...]), 0.0)
-    prob[...] = loss_scale * (index_prob - prob[...] / row_total)
+    row_total = jnp.sum(jnp.where(diagonal, jnp.broadcast_to(row[:1], square), 0.0), axis=1, keepdims=True)
+    prob[...] = jnp.broadcast_to(row_total, (count, keys))
+    for k in range(peers):
+        part = pl.ds(pl.multiple_of(jnp.bitwise_xor(info[1], k) * size, size), size)
+        target = slices[k][...].astype(F32) / prob[part, :]
+        prob[part, :] = loss_scale * (index_slices[k][...].astype(F32) - target)
 
     weight = jnp.concatenate([w_a[...], w_b[...]], axis=0).astype(F32)
     for j in range(heads):
@@ -264,17 +279,22 @@
     info = jnp.stack([key_blocks[0], lax.axis_index("head").astype(jnp.int32)])
     evens = list(range(2, ctx, 2))
 
-    payload = jnp.concatenate(
-        [
-            query_heads[:, :, :nope].reshape(chunk, -1),
-            query_heads[:, :, nope:].reshape(chunk, -1),
-            index_query.reshape(chunk, -1),
-            jnp.pad(index_weight, ((0, 0), (0, LANES - index_heads))),
-        ],
-        axis=1,
-    )
-    side_a = jnp.concatenate([payload] + [send(payload, "ctx", ctx, k) for k in evens], axis=0)
-    side_b = send(side_a, "ctx", ctx, 1)
+    def gather(payload):
+        side = jnp.concatenate([payload] + [send(payload, "ctx", ctx, k) for k in evens], axis=0)
+        return side, send(side, "ctx", ctx, 1)
+
+    index_a, index_b = gather(
+        jnp.concatenate(
+            [index_query.reshape(chunk, -1), jnp.pad(index_weight, ((0, 0), (0, LANES - index_heads)))],
+            axis=1,
+        )
+    )
+    side_a, side_b = gather(
+        jnp.concatenate(
+            [query_heads[:, :, :nope].reshape(chunk, -1), query_heads[:, :, nope:].reshape(chunk, -1)],
+            axis=1,
+        )
+    )
 
     local = jnp.concatenate(
         [lse_heads * LOG2E, lse_index[:, None], query_pos.astype(F32)[:, None]], axis=1
@@ -290,25 +310,31 @@
     index_t = index_keys.T
 
     iq_width = index_heads * depth
-    iq_spec = pl.BlockSpec((half, iq_width), lambda *_: (0, heads * width // iq_width))
-    w_spec = pl.BlockSpec((half, LANES), lambda *_: (0, (heads * width + iq_width) // LANES))
-    logit_part = call(
+    iq_spec = pl.BlockSpec((half, iq_width), lambda *_: (0, 0))
+    w_spec = pl.BlockSpec((half, LANES), lambda *_: (0, iq_width // LANES))
+    part_rows = count // peers
+    logit_slices = call(
         logit_kernel,
-        jax.ShapeDtypeStruct((count, keys), F32),
+        [jax.ShapeDtypeStruct((part_rows, keys), F32)] * peers,
         grid=(1,),
-        in_specs=[iq_spec, iq_spec, w_spec, w_spec, vmem()],
+        in_specs=[smem(), iq_spec, iq_spec, w_spec, w_spec, vmem()],
+        out_specs=[vmem()] * peers,
+        scratch_shapes=[pltpu.VMEM((index_heads * count, depth), BF16), pltpu.VMEM((count, keys), F32)],
+    )(info, index_a, index_b, index_a, index_b, index_t)
+    index_prob = call(
+        index_prob_kernel,
+        jax.ShapeDtypeStruct((part_rows, keys), BF16),
+        in_specs=[smem()] + [vmem()] * (peers + 2),
         out_specs=vmem(),
-        scratch_shapes=[pltpu.VMEM((index_heads * count, depth), BF16)],
-    )(side_a, side_b, side_a, side_b, index_t)
-    logits = lax.psum(logit_part, "head")
+    )(info, lse_column, pos_column, *swap_heads(logit_slices, peers))
+    index_probs = swap_heads([index_prob] * peers, peers)
 
     rope_first = heads * nope // (group * rope)
     nope_spec = pl.BlockSpec((half, group * nope), lambda g: (0, g))
     rope_spec = pl.BlockSpec((half, group * rope), lambda g: (0, rope_first + g))
-    slice_shape = jax.ShapeDtypeStruct((count // peers, keys), BF16)
-    *slices, row_sum = call(
+    slices = call(
         functools.partial(prob_kernel, width ** -0.5),
-        [slice_shape] * peers + [jax.ShapeDtypeStruct((8, count), F32)],
+        [jax.ShapeDtypeStruct((part_rows, keys + count), BF16)] * peers,
         grid=(steps,),
         in_specs=[
             smem(),
@@ -321,29 +347,28 @@
             pl.BlockSpec((1, count, group), lambda g: (g, 0, 0)),
             vmem(),
         ],
-        out_specs=[vmem()] * (peers + 1),
+        out_specs=[vmem()] * peers,
         scratch_shapes=[
             pltpu.VMEM((group * count, latent + LANES), BF16),
             pltpu.VMEM((count, keys), F32),
         ],
     )(info, side_a, side_b, side_a, side_b, absorb_up, latent_t, lse_groups, pos_column)
 
+    merged, row_sum = call(
+        merge_kernel,
+        [jax.ShapeDtypeStruct((part_rows, keys), BF16), jax.ShapeDtypeStruct((8, count), F32)],
+    )(*swap_heads(slices, peers))
     row_sum = call(
         functools.partial(add_swapped_kernel, chunk),
         jax.ShapeDtypeStruct((8, count), F32),
     )(row_sum, send(row_sum, "ctx", ctx, 1))
-    got = [slices[0]] + [send(slices[k], "head", peers, k) for k in range(1, peers)]
     totals = [row_sum] + [send(row_sum, "ctx", ctx, k) for k in evens]
-    merged = call(
-        functools.partial(merge_kernel, chunk, peers, evens),
-        jax.ShapeDtypeStruct((count // peers + 16, keys), BF16),
-    )(*got, *totals)
-    gathered = [merged] + [send(merged, "head", peers, k) for k in range(1, peers)]
+    gathered = swap_heads([merged] * peers, peers)
 
     loss_scale = (keys * ctx) ** 0.5
     dk_slice = (keys // peers, depth)
     outs = call(
-        functools.partial(grad_kernel, loss_scale, peers),
+        functools.partial(grad_kernel, loss_scale, chunk, peers, evens),
         [
             jax.ShapeDtypeStruct((half, iq_width), F32),
             jax.ShapeDtypeStruct((half, iq_width), BF16),
@@ -352,8 +377,8 @@
         + [jax.ShapeDtypeStruct(dk_slice, BF16)] * (peers - 1),
         grid=(1,),
         in_specs=[smem()]
-        + [vmem()] * peers
-        + [vmem(), iq_spec, iq_spec, w_spec, w_spec, vmem(), vmem(), vmem(), vmem()],
+        + [vmem()] * (2 * peers + len(totals))
+        + [iq_spec, iq_spec, w_spec, w_spec, vmem(), vmem()],
         out_specs=[vmem()] * (peers + 2),
         scratch_shapes=[
             pltpu.VMEM((index_heads * count, depth), BF16),
@@ -363,19 +388,18 @@
     )(
         info,
         *gathered,
-        logits,
-        side_a,
-        side_b,
-        side_a,
-        side_b,
+        *index_probs,
+        *totals,
+        index_a,
+        index_b,
+        index_a,
+        index_b,
         index_keys,
         index_t,
-        lse_column,
-        pos_column,
     )
     keep, away, dk_own, *dk_away = outs
     other = send(away, "ctx", ctx, 1)
-    dk_parts = [dk_own] + [send(dk_away[k - 1], "head", peers, k) for k in range(1, peers)]
+    dk_parts = swap_heads([dk_own] + dk_away, peers)
     own, *parts = call(
         fold_kernel,
         [jax.ShapeDtypeStruct((chunk, iq_width), F32)]

time: 106 us -> 82.6 us (0.78)
  between operations: 15 us -> 1.72 us
  starting transfers between devices: 26.6 us -> 38.3 us
  waiting for transfers between devices: 25.3 us -> 16.6 us
  Pallas kernels: 27 us -> 18.5 us
  local copies, waits for them, and re-layouts: 10.1 us -> 5.83 us
    ppermute x21 -> x31, starting transfers between devices: 26.6 us -> 38.3 us  [send(): return lax.ppermute(array, axis, [(i, i ^ offset) for i in range(size)])]
    ppermute x21 -> x31, waiting for transfers between devices: 25.3 us -> 16.6 us  [send(): return lax.ppermute(array, axis, [(i, i ^ offset) for i in range(size)])]
    pallas_call x4 -> x5, Pallas kernels: 26.1 us -> 17.6 us  [the longest x1 10.3 us: body(): call(functools.partial(prob_kernel, width ** (-0.5)), [jax.ShapeDtypeStru...]
    concatenate x8, local copies, waits for them, and re-layouts: 3.56 us -> 1.61 us  [body(): jnp.concatenate([lse_heads * LOG2E, lse_index[:, None], query_pos.astype(...]
    transpose x1, local copies, waits for them, and re-layouts: 1.38 us -> 0.11 us  [body(): latent_t = jnp.pad(latent_keys, ((0, 0), (0, LANES - rope))).T]
  transfers between devices with their start and end apart: 22 -> 31, of which waited for: 11 -> 13; matrix products, arithmetic and copies ran while one was open for 6% -> 6% of each run, Pallas kernels for 18% -> 16%
where the time goes in v2:
time: 82.6 us; the launch traced here: 82.3 us
  starting transfers between devices  38.3 us (46%)
  Pallas kernels  18.5 us (22%)
  waiting for transfers between devices  16.6 us (20%)
  local copies, waits for them, and re-layouts  5.83 us (7%)
  between operations  1.72 us (2%)
  other arithmetic  1.33 us (2%)
    ppermute x31, starting transfers between devices, send(): return lax.ppermute(array, axis, [(i, i ^ offset) for i in range(size)])  38.3 us
    ppermute x31, waiting for transfers between devices, send(): return lax.ppermute(array, axis, [(i, i ^ offset) for i in range(size)])  16.6 us
    pallas_call x1, Pallas kernels, body(): call(functools.partial(prob_kernel, width ** (-0.5)), [jax.ShapeDtypeStru...  10.3 us
    pallas_call x1, Pallas kernels, body(): call(functools.partial(grad_kernel, loss_scale, chunk, peers, evens), [ja...  4.72 us
    pallas_call x1, Pallas kernels, body(): call(logit_kernel, [jax.ShapeDtypeStruct((part_rows, keys), F32)] * peers...  1.83 us
  transfers between devices with their start and end apart: 31, of which 13 were waited for; matrix products, arithmetic and copies ran while one was open for 6% of the time, Pallas kernels for 16%

profile of v2, /device:TPU:0, one launch (start us, length us, event | category | flops | bytes accessed | tf_op | source)
XLA Modules:
  0.0 82.3 jit_solution(11696431470771729353)
XLA Ops:
  0.6 0.9 %slice.15 = bf16[16,32,128]{2,1,0:T(8,128)(2,1)S(1)} slice(bf16[16,32,192]{2,1,0:T(8,128)(2,1)} %param.10), slice={[0:16], [0:32], [0:128]} | slice | bytes 262144 | tf_op jit(solution)/shard_map/slice | solution.py:294
  1.6 0.9 %slice.16 = bf16[16,32,64]{2,1,0:T(8,128)(2,1)S(1)} slice(bf16[16,32,192]{2,1,0:T(8,128)(2,1)} %param.10), slice={[0:16], [0:32], [128:192]} | slice | bytes 131072 | tf_op jit(solution)/shard_map/slice | solution.py:294
  2.7 3.0 %collective-permute-start = (bf16[16,6144]{1,0:T(8,128)(2,1)S(1)}, bf16[16,6144]{1,0:T(8,128)(2,1)S(1)}, u32[]{:S(2)}, u32[]{:S(2)}) collective-permute-start(bf16[16,6144]{1,0:T(8,128)(2,1)S(1)} %constant_dynamic-update-slice_fusion), channel_id=1, source_target_pairs={{0,8},{4,12},{8,0},{12,4},{16,24},{20,28},{24,16},{28,20},{1,9},{5... | collective-permute-start | bytes 589832 | tf_op jit(solution)/shard_map/ppermute | solution.py:23
  5.8 1.5 %collective-permute-start.1 = (bf16[16,6144]{1,0:T(8,128)(2,1)S(1)}, bf16[16,6144]{1,0:T(8,128)(2,1)S(1)}, u32[]{:S(2)}, u32[]{:S(2)}) collective-permute-start(bf16[16,6144]{1,0:T(8,128)(2,1)S(1)} %constant_dynamic-update-slice_fusion), channel_id=1, source_target_pairs={{0,16},{4,20},{8,24},{12,28},{16,0},{20,4},{24,8},{28,12},{1,17},{... | collective-permute-start | bytes 589832 | tf_op jit(solution)/shard_map/ppermute | solution.py:23
  7.3 0.9 %copy.39 = bf16[2,8,16,128]{3,1,2,0:T(8,128)(2,1)S(1)} copy(bf16[2,8,16,128]{3,2,1,0:T(8,128)(2,1)} %bitcast.46) | data formatting | bytes 131072
  8.2 0.7 pad.9
  8.9 2.0 %collective-permute-start.10 = (bf16[16,2176]{1,0:T(8,128)(2,1)S(1)}, bf16[16,2176]{1,0:T(8,128)(2,1)S(1)}, u32[]{:S(2)}, u32[]{:S(2)}) collective-permute-start(bf16[16,2176]{1,0:T(8,128)(2,1)S(1)} %pad_maximum_fusion.2), channel_id=1, source_target_pairs={{0,8},{4,12},{8,0},{12,4},{16,24},{20,28},{24,16},{28,20},{1,9},{5... | collective-permute-start | bytes 208904 | tf_op jit(solution)/shard_map/ppermute | solution.py:23
  10.9 1.5 %collective-permute-start.11 = (bf16[16,2176]{1,0:T(8,128)(2,1)S(1)}, bf16[16,2176]{1,0:T(8,128)(2,1)S(1)}, u32[]{:S(2)}, u32[]{:S(2)}) collective-permute-start(bf16[16,2176]{1,0:T(8,128)(2,1)S(1)} %pad_maximum_fusion.2), channel_id=1, source_target_pairs={{0,16},{4,20},{8,24},{12,28},{16,0},{20,4},{24,8},{28,12},{1,17},{... | collective-permute-start | bytes 208904 | tf_op jit(solution)/shard_map/ppermute | solution.py:23
  12.4 0.7 convert_element_type.10
  13.7 0.2 concatenate.78
  13.9 0.2 concatenate.81
  16.2 0.8 collective-permute-done.1
  17.1 0.7 collective-permute-done.11
  17.8 3.5 %collective-permute-done.12 = bf16[16,2176]{1,0:T(8,128)(2,1)S(1)} collective-permute-done((bf16[16,2176]{1,0:T(8,128)(2,1)S(1)}, bf16[16,2176]{1,0:T(8,128)(2,1)S(1)}, u32[]{:S(2)}, u32[]{:S(2)}) %collective-permute-start.12) | collective-permute-done | bytes 69664 | tf_op jit(solution)/shard_map/ppermute | solution.py:23
  22.0 1.0 %collective-permute-done.13.iq_b.w_b.refs_13_.refs_15_ = bf16[64,2176]{1,0:T(8,128)(2,1)S(1)} collective-permute-done((bf16[64,2176]{1,0:T(8,128)(2,1)S(1)}, bf16[64,2176]{1,0:T(8,128)(2,1)S(1)}, u32[]{:S(2)}, u32[]{:S(2)}) %collective-permute-start.13) | collective-permute-done | bytes 278560 | tf_op jit(solution)/shard_map/ppermute | solution.py:23
  23.0 1.8 %shard_map.115 = (f32[32,1024]{1,0:T(8,128)S(1)}, f32[32,1024]{1,0:T(8,128)S(1)}, f32[32,1024]{1,0:T(8,128)S(1)}, f32[32,1024]{1,0:T(8,128)S(1)}) custom-call(s32[2]{0:T(128)S(1)} %pad_add_fusion.info, bf16[64,2176]{1,0:T(8,128)(2,1)S(1)} %pad_maximum_fusion.1.iq_a.w_a.refs_12_.refs_14_, ...), custom_call_target="tpu_custom_call" | custom-call | tf_op jit(solution)/shard_map/pallas_call | solution.py:316
  24.8 1.6 %collective-permute-start.14 = (f32[32,1024]{1,0:T(8,128)S(1)}, f32[32,1024]{1,0:T(8,128)S(1)}, u32[]{:S(2)}, u32[]{:S(2)}) collective-permute-start(f32[32,1024]{1,0:T(8,128)S(1)} %get-tuple-element.28), channel_id=1, source_target_pairs={{0,1},{1,0},{2,3},{3,2},{4,5},{5,4},{6,7},{7,6},{8,9},{9,8},{10,11... | collective-permute-start | bytes 393224 | tf_op jit(solution)/shard_map/ppermute | solution.py:23
  26.5 2.6 %collective-permute-start.15 = (f32[32,1024]{1,0:T(8,128)S(1)}, f32[32,1024]{1,0:T(8,128)S(1)}, u32[]{:S(2)}, u32[]{:S(2)}) collective-permute-start(f32[32,1024]{1,0:T(8,128)S(1)} %get-tuple-element.29), channel_id=1, source_target_pairs={{0,2},{1,3},{2,0},{3,1},{4,6},{5,7},{6,4},{7,5},{8,10},{9,11},{10,... | collective-permute-start | bytes 393224 | tf_op jit(solution)/shard_map/ppermute | solution.py:23
  29.1 0.2 collective-permute-start.16
  29.4 10.3 %shard_map.113 = (bf16[32,1152]{1,0:T(8,128)(2,1)S(1)}, bf16[32,1152]{1,0:T(8,128)(2,1)S(1)}, bf16[32,1152]{1,0:T(8,128)(2,1)S(1)}, bf16[32,1152]{1,0:T(8,128)(2,1)S(1)}) custom-call(s32[2]{0:T(128)S(1)} %pad_add_fusion.info, bf16[64,6144]{1,0:T(8,128)(2,1)S(1)} %pad_maximum_fusion.na.ra, bf16[64,6144]{1,0:T(8,128)(2,1)S(1)} %collective-permute-done.3.nb.rb, ...), custom_call_target="tpu_custom_call" | custom-call | tf_op jit(solution)/shard_map/pallas_call | solution.py:335
  39.8 0.7 collective-permute-start.4
  40.5 3.5 %collective-permute-start.5 = (bf16[32,1152]{1,0:T(8,128)(2,1)S(1)}, bf16[32,1152]{1,0:T(8,128)(2,1)S(1)}, u32[]{:S(2)}, u32[]{:S(2)}) collective-permute-start(bf16[32,1152]{1,0:T(8,128)(2,1)S(1)} %get-tuple-element.24), channel_id=1, source_target_pairs={{0,2},{1,3},{2,0},{3,1},{4,6},{5,7},{6,4},{7,5},{8,10},{9,11},{10,... | collective-permute-start | bytes 221192 | tf_op jit(solution)/shard_map/ppermute | solution.py:23
  44.0 0.2 collective-permute-start.6
  44.2 0.6 shard_map.116.refs_4_
  44.9 0.4 collective-permute-start.17
  45.3 3.8 %collective-permute-start.18 = (bf16[32,1024]{1,0:T(8,128)(2,1)S(1)}, bf16[32,1024]{1,0:T(8,128)(2,1)S(1)}, u32[]{:S(2)}, u32[]{:S(2)}) collective-permute-start(bf16[32,1024]{1,0:T(8,128)(2,1)S(1)} %shard_map.116.refs_4_), channel_id=1, source_target_pairs={{0,2},{1,3},{2,0},{3,1},{4,6},{5,7},{6,4},{7,5},{8,10},{9,11},{10,... | collective-permute-start | bytes 196616 | tf_op jit(solution)/shard_map/ppermute | solution.py:23
  49.1 0.2 collective-permute-start.19
  49.3 0.9 %collective-permute-done.5.refs_2_ = bf16[32,1152]{1,0:T(8,128)(2,1)S(1)} collective-permute-done((bf16[32,1152]{1,0:T(8,128)(2,1)S(1)}, bf16[32,1152]{1,0:T(8,128)(2,1)S(1)}, u32[]{:S(2)}, u32[]{:S(2)}) %collective-permute-start.5) | collective-permute-done | bytes 73760 | tf_op jit(solution)/shard_map/ppermute | solution.py:23
  50.4 3.6 %collective-permute-start.7 = (bf16[32,1024]{1,0:T(8,128)(2,1)S(1)}, bf16[32,1024]{1,0:T(8,128)(2,1)S(1)}, u32[]{:S(2)}, u32[]{:S(2)}) collective-permute-start(bf16[32,1024]{1,0:T(8,128)(2,1)S(1)} %get-tuple-element.26.refs_0_), channel_id=1, source_target_pairs={{0,1},{1,0},{2,3},{3,2},{4,5},{5,4},{6,7},{7,6},{8,9},{9,8},{10,11... | collective-permute-start | bytes 196616 | tf_op jit(solution)/shard_map/ppermute | solution.py:23
  54.0 2.1 %collective-permute-start.8 = (bf16[32,1024]{1,0:T(8,128)(2,1)S(1)}, bf16[32,1024]{1,0:T(8,128)(2,1)S(1)}, u32[]{:S(2)}, u32[]{:S(2)}) collective-permute-start(bf16[32,1024]{1,0:T(8,128)(2,1)S(1)} %get-tuple-element.26.refs_0_), channel_id=1, source_target_pairs={{0,2},{1,3},{2,0},{3,1},{4,6},{5,7},{6,4},{7,5},{8,10},{9,11},{10,... | collective-permute-start | bytes 196616 | tf_op jit(solution)/shard_map/ppermute | solution.py:23
  56.1 1.4 %collective-permute-start.9 = (bf16[32,1024]{1,0:T(8,128)(2,1)S(1)}, bf16[32,1024]{1,0:T(8,128)(2,1)S(1)}, u32[]{:S(2)}, u32[]{:S(2)}) collective-permute-start(bf16[32,1024]{1,0:T(8,128)(2,1)S(1)} %get-tuple-element.26.refs_0_), channel_id=1, source_target_pairs={{0,3},{1,2},{2,1},{3,0},{4,7},{5,6},{6,5},{7,4},{8,11},{9,10},{10,... | collective-permute-start | bytes 196616 | tf_op jit(solution)/shard_map/ppermute | solution.py:23
  57.6 0.5 collective-permute-start.21
  58.2 0.5 collective-permute-start.22
  58.7 2.6 %collective-permute-done.21.refs_9_ = f32[8,128]{1,0:T(8,128)S(1)} collective-permute-done((f32[8,128]{1,0:T(8,128)S(1)}, f32[8,128]{1,0:T(8,128)S(1)}, u32[]{:S(2)}, u32[]{:S(2)}) %collective-permute-start.21) | collective-permute-done | bytes 4128 | tf_op jit(solution)/shard_map/ppermute | solution.py:23
  61.2 0.5 collective-permute-start.23
  61.8 4.0 %collective-permute-done.23.refs_11_ = f32[8,128]{1,0:T(8,128)S(1)} collective-permute-done((f32[8,128]{1,0:T(8,128)S(1)}, f32[8,128]{1,0:T(8,128)S(1)}, u32[]{:S(2)}, u32[]{:S(2)}) %collective-permute-start.23) | collective-permute-done | bytes 4128 | tf_op jit(solution)/shard_map/ppermute | solution.py:23
  65.8 4.7 %shard_map.118 = (f32[64,2048]{1,0:T(8,128)S(1)}, bf16[64,2048]{1,0:T(8,128)(2,1)S(1)}, f32[256,128]{1,0:T(8,128)S(1)}, bf16[256,128]{1,0:T(8,128)(2,1)S(1)}, bf...) custom-call(s32[2]{0:T(128)S(1)} %pad_add_fusion.info, bf16[32,1024]{1,0:T(8,128)(2,1)S(1)} %get-tuple-element.26.refs_0_, ...), custom_call_target="tpu_custom_call" | custom-call | tf_op jit(solution)/shard_map/pallas_call | solution.py:370
  70.6 0.6 collective-permute-start.28
  71.1 2.4 %collective-permute-start.29 = (bf16[256,128]{1,0:T(8,128)(2,1)S(1)}, bf16[256,128]{1,0:T(8,128)(2,1)S(1)}, u32[]{:S(2)}, u32[]{:S(2)}) collective-permute-start(bf16[256,128]{1,0:T(8,128)(2,1)S(1)} %get-tuple-element.40), channel_id=1, source_target_pairs={{0,2},{1,3},{2,0},{3,1},{4,6},{5,7},{6,4},{7,5},{8,10},{9,11},{10,... | collective-permute-start | bytes 196616 | tf_op jit(solution)/shard_map/ppermute | solution.py:23
  73.6 1.4 %collective-permute-start.30 = (bf16[256,128]{1,0:T(8,128)(2,1)S(1)}, bf16[256,128]{1,0:T(8,128)(2,1)S(1)}, u32[]{:S(2)}, u32[]{:S(2)}) collective-permute-start(bf16[256,128]{1,0:T(8,128)(2,1)S(1)} %get-tuple-element.41), channel_id=1, source_target_pairs={{0,3},{1,2},{2,1},{3,0},{4,7},{5,6},{6,5},{7,4},{8,11},{9,10},{10,... | collective-permute-start | bytes 196616 | tf_op jit(solution)/shard_map/ppermute | solution.py:23
  75.1 0.6 collective-permute-start.25
  75.7 0.5 collective-permute-start.26
  76.4 2.3 %collective-permute-start.27 = (bf16[16,2048]{1,0:T(8,128)(2,1)S(1)}, bf16[16,2048]{1,0:T(8,128)(2,1)S(1)}, u32[]{:S(2)}, u32[]{:S(2)}) collective-permute-start(bf16[16,2048]{1,0:T(8,128)(2,1)S(1)} %get-tuple-element.37), channel_id=1, source_target_pairs={{0,24},{4,28},{8,16},{12,20},{16,8},{20,12},{24,0},{28,4},{1,25},{... | collective-permute-start | bytes 196616 | tf_op jit(solution)/shard_map/ppermute | solution.py:23
  78.7 1.0 %collective-permute-done.30.refs_7_ = bf16[256,128]{1,0:T(8,128)(2,1)S(1)} collective-permute-done((bf16[256,128]{1,0:T(8,128)(2,1)S(1)}, bf16[256,128]{1,0:T(8,128)(2,1)S(1)}, u32[]{:S(2)}, u32[]{:S(2)}) %collective-permute-start.30) | collective-permute-done | bytes 65568 | tf_op jit(solution)/shard_map/ppermute | solution.py:23
  79.7 0.3 collective-permute-done.25.refs_1_
  80.0 0.4 collective-permute-done.26.refs_2_
  80.4 1.1 %collective-permute-done.27.refs_3_ = bf16[16,2048]{1,0:T(8,128)(2,1)S(1)} collective-permute-done((bf16[16,2048]{1,0:T(8,128)(2,1)S(1)}, bf16[16,2048]{1,0:T(8,128)(2,1)S(1)}, u32[]{:S(2)}, u32[]{:S(2)}) %collective-permute-start.27) | collective-permute-done | bytes 65568 | tf_op jit(solution)/shard_map/ppermute | solution.py:23
  81.5 0.8 shard_map.120
  (65 shorter events, 3.6 us)
Async XLA Ops:
  0.6 12.8 %copy-start.3 = (f32[128]{0:T(128)S(1)}, f32[128]{0:T(128)}, u32[]{:S(2)}) copy-start(f32[128]{0:T(128)} %param.17) | copy-start | bytes 1540
  0.6 14.1 %copy-start.2 = (f32[128,32]{0,1:T(8,128)S(1)}, f32[128,32]{0,1:T(8,128)}, u32[]{:S(2)}) copy-start(f32[128,32]{0,1:T(8,128)} %param.13) | copy-start | bytes 49156
  2.7 13.3 %collective-permute-start = (bf16[16,6144]{1,0:T(8,128)(2,1)S(1)}, bf16[16,6144]{1,0:T(8,128)(2,1)S(1)}, u32[]{:S(2)}, u32[]{:S(2)}) collective-permute-start(bf16[16,6144]{1,0:T(8,128)(2,1)S(1)} %constant_dynamic-update-slice_fusion), channel_id=1, source_target_pairs={{0,8},{4,12},{8,0},{12,4},{16,24},{20,28},{24,16},{28,20},{1,9},{5... | collective-permute-start | bytes 589832 | tf_op jit(solution)/shard_map/ppermute | solution.py:23
  5.8 11.2 %collective-permute-start.1 = (bf16[16,6144]{1,0:T(8,128)(2,1)S(1)}, bf16[16,6144]{1,0:T(8,128)(2,1)S(1)}, u32[]{:S(2)}, u32[]{:S(2)}) collective-permute-start(bf16[16,6144]{1,0:T(8,128)(2,1)S(1)} %constant_dynamic-update-slice_fusion), channel_id=1, source_target_pairs={{0,16},{4,20},{8,24},{12,28},{16,0},{20,4},{24,8},{28,12},{1,17},{... | collective-permute-start | bytes 589832 | tf_op jit(solution)/shard_map/ppermute | solution.py:23
  7.3 9.7 %collective-permute-start.2 = (bf16[16,6144]{1,0:T(8,128)(2,1)S(1)}, bf16[16,6144]{1,0:T(8,128)(2,1)S(1)}, u32[]{:S(2)}, u32[]{:S(2)}) collective-permute-start(bf16[16,6144]{1,0:T(8,128)(2,1)S(1)} %constant_dynamic-update-slice_fusion), channel_id=1, source_target_pairs={{0,24},{4,28},{8,16},{12,20},{16,8},{20,12},{24,0},{28,4},{1,25},{... | collective-permute-start | bytes 589832 | tf_op jit(solution)/shard_map/ppermute | solution.py:23
  8.9 8.2 %collective-permute-start.10 = (bf16[16,2176]{1,0:T(8,128)(2,1)S(1)}, bf16[16,2176]{1,0:T(8,128)(2,1)S(1)}, u32[]{:S(2)}, u32[]{:S(2)}) collective-permute-start(bf16[16,2176]{1,0:T(8,128)(2,1)S(1)} %pad_maximum_fusion.2), channel_id=1, source_target_pairs={{0,8},{4,12},{8,0},{12,4},{16,24},{20,28},{24,16},{28,20},{1,9},{5... | collective-permute-start | bytes 208904 | tf_op jit(solution)/shard_map/ppermute | solution.py:23
  10.9 6.9 %collective-permute-start.11 = (bf16[16,2176]{1,0:T(8,128)(2,1)S(1)}, bf16[16,2176]{1,0:T(8,128)(2,1)S(1)}, u32[]{:S(2)}, u32[]{:S(2)}) collective-permute-start(bf16[16,2176]{1,0:T(8,128)(2,1)S(1)} %pad_maximum_fusion.2), channel_id=1, source_target_pairs={{0,16},{4,20},{8,24},{12,28},{16,0},{20,4},{24,8},{28,12},{1,17},{... | collective-permute-start | bytes 208904 | tf_op jit(solution)/shard_map/ppermute | solution.py:23
  15.2 6.5 %copy-start = (bf16[1024,128]{1,0:T(8,128)(2,1)S(1)}, bf16[1024,128]{1,0:T(8,128)(2,1)}, u32[]{:S(2)}) copy-start(bf16[1024,128]{1,0:T(8,128)(2,1)} %refs_16_.1) | copy-start | bytes 786436
  16.1 5.3 %collective-permute-start.12 = (bf16[16,2176]{1,0:T(8,128)(2,1)S(1)}, bf16[16,2176]{1,0:T(8,128)(2,1)S(1)}, u32[]{:S(2)}, u32[]{:S(2)}) collective-permute-start(bf16[16,2176]{1,0:T(8,128)(2,1)S(1)} %pad_maximum_fusion.2), channel_id=1, source_target_pairs={{0,24},{4,28},{8,16},{12,20},{16,8},{20,12},{24,0},{28,4},{1,25},{... | collective-permute-start | bytes 208904 | tf_op jit(solution)/shard_map/ppermute | solution.py:23
  17.0 12.4 %collective-permute-start.3 = (bf16[64,6144]{1,0:T(8,128)(2,1)S(1)}, bf16[64,6144]{1,0:T(8,128)(2,1)S(1)}, u32[]{:S(2)}, u32[]{:S(2)}) collective-permute-start(bf16[64,6144]{1,0:T(8,128)(2,1)S(1)} %pad_maximum_fusion.na.ra), channel_id=1, source_target_pairs={{0,4},{4,0},{8,12},{12,8},{16,20},{20,16},{24,28},{28,24},{1,5},{5... | collective-permute-start | bytes 2359304 | tf_op jit(solution)/shard_map/ppermute | solution.py:23
  21.4 1.6 %collective-permute-start.13 = (bf16[64,2176]{1,0:T(8,128)(2,1)S(1)}, bf16[64,2176]{1,0:T(8,128)(2,1)S(1)}, u32[]{:S(2)}, u32[]{:S(2)}) collective-permute-start(bf16[64,2176]{1,0:T(8,128)(2,1)S(1)} %pad_maximum_fusion.1.iq_a.w_a.refs_12_.refs_14_), channel_id=1, source_target_pairs={{0,4},{4,0},{8,12},{12,8},{16,20},{20,16},{24,28},{28,24},{1,5},{5... | collective-permute-start | bytes 835592 | tf_op jit(solution)/shard_map/ppermute | solution.py:23
  21.9 7.4 %copy-start.1 = (bf16[1024,576]{0,1:T(8,128)(2,1)S(1)}, bf16[1024,576]{0,1:T(8,128)(2,1)}, u32[]{:S(2)}) copy-start(bf16[1024,576]{0,1:T(8,128)(2,1)} %param.12) | copy-start | bytes 3538948
  24.8 19.2 %collective-permute-start.14 = (f32[32,1024]{1,0:T(8,128)S(1)}, f32[32,1024]{1,0:T(8,128)S(1)}, u32[]{:S(2)}, u32[]{:S(2)}) collective-permute-start(f32[32,1024]{1,0:T(8,128)S(1)} %get-tuple-element.28), channel_id=1, source_target_pairs={{0,1},{1,0},{2,3},{3,2},{4,5},{5,4},{6,7},{7,6},{8,9},{9,8},{10,11... | collective-permute-start | bytes 393224 | tf_op jit(solution)/shard_map/ppermute | solution.py:23
  26.5 17.7 %collective-permute-start.15 = (f32[32,1024]{1,0:T(8,128)S(1)}, f32[32,1024]{1,0:T(8,128)S(1)}, u32[]{:S(2)}, u32[]{:S(2)}) collective-permute-start(f32[32,1024]{1,0:T(8,128)S(1)} %get-tuple-element.29), channel_id=1, source_target_pairs={{0,2},{1,3},{2,0},{3,1},{4,6},{5,7},{6,4},{7,5},{8,10},{9,11},{10,... | collective-permute-start | bytes 393224 | tf_op jit(solution)/shard_map/ppermute | solution.py:23
  29.1 15.1 %collective-permute-start.16 = (f32[32,1024]{1,0:T(8,128)S(1)}, f32[32,1024]{1,0:T(8,128)S(1)}, u32[]{:S(2)}, u32[]{:S(2)}) collective-permute-start(f32[32,1024]{1,0:T(8,128)S(1)} %get-tuple-element.30), channel_id=1, source_target_pairs={{0,3},{1,2},{2,1},{3,0},{4,7},{5,6},{6,5},{7,4},{8,11},{9,10},{10,... | collective-permute-start | bytes 393224 | tf_op jit(solution)/shard_map/ppermute | solution.py:23
  39.8 9.4 %collective-permute-start.4 = (bf16[32,1152]{1,0:T(8,128)(2,1)S(1)}, bf16[32,1152]{1,0:T(8,128)(2,1)S(1)}, u32[]{:S(2)}, u32[]{:S(2)}) collective-permute-start(bf16[32,1152]{1,0:T(8,128)(2,1)S(1)} %get-tuple-element.23), channel_id=1, source_target_pairs={{0,1},{1,0},{2,3},{3,2},{4,5},{5,4},{6,7},{7,6},{8,9},{9,8},{10,11... | collective-permute-start | bytes 221192 | tf_op jit(solution)/shard_map/ppermute | solution.py:23
  40.5 9.8 %collective-permute-start.5 = (bf16[32,1152]{1,0:T(8,128)(2,1)S(1)}, bf16[32,1152]{1,0:T(8,128)(2,1)S(1)}, u32[]{:S(2)}, u32[]{:S(2)}) collective-permute-start(bf16[32,1152]{1,0:T(8,128)(2,1)S(1)} %get-tuple-element.24), channel_id=1, source_target_pairs={{0,2},{1,3},{2,0},{3,1},{4,6},{5,7},{6,4},{7,5},{8,10},{9,11},{10,... | collective-permute-start | bytes 221192 | tf_op jit(solution)/shard_map/ppermute | solution.py:23
  44.0 6.3 %collective-permute-start.6 = (bf16[32,1152]{1,0:T(8,128)(2,1)S(1)}, bf16[32,1152]{1,0:T(8,128)(2,1)S(1)}, u32[]{:S(2)}, u32[]{:S(2)}) collective-permute-start(bf16[32,1152]{1,0:T(8,128)(2,1)S(1)} %get-tuple-element.25), channel_id=1, source_target_pairs={{0,3},{1,2},{2,1},{3,0},{4,7},{5,6},{6,5},{7,4},{8,11},{9,10},{10,... | collective-permute-start | bytes 221192 | tf_op jit(solution)/shard_map/ppermute | solution.py:23
  44.9 9.1 %collective-permute-start.17 = (bf16[32,1024]{1,0:T(8,128)(2,1)S(1)}, bf16[32,1024]{1,0:T(8,128)(2,1)S(1)}, u32[]{:S(2)}, u32[]{:S(2)}) collective-permute-start(bf16[32,1024]{1,0:T(8,128)(2,1)S(1)} %shard_map.116.refs_4_), channel_id=1, source_target_pairs={{0,1},{1,0},{2,3},{3,2},{4,5},{5,4},{6,7},{7,6},{8,9},{9,8},{10,11... | collective-permute-start | bytes 196616 | tf_op jit(solution)/shard_map/ppermute | solution.py:23
  45.3 12.4 %collective-permute-start.18 = (bf16[32,1024]{1,0:T(8,128)(2,1)S(1)}, bf16[32,1024]{1,0:T(8,128)(2,1)S(1)}, u32[]{:S(2)}, u32[]{:S(2)}) collective-permute-start(bf16[32,1024]{1,0:T(8,128)(2,1)S(1)} %shard_map.116.refs_4_), channel_id=1, source_target_pairs={{0,2},{1,3},{2,0},{3,1},{4,6},{5,7},{6,4},{7,5},{8,10},{9,11},{10,... | collective-permute-start | bytes 196616 | tf_op jit(solution)/shard_map/ppermute | solution.py:23
  49.1 9.1 %collective-permute-start.19 = (bf16[32,1024]{1,0:T(8,128)(2,1)S(1)}, bf16[32,1024]{1,0:T(8,128)(2,1)S(1)}, u32[]{:S(2)}, u32[]{:S(2)}) collective-permute-start(bf16[32,1024]{1,0:T(8,128)(2,1)S(1)} %shard_map.116.refs_4_), channel_id=1, source_target_pairs={{0,3},{1,2},{2,1},{3,0},{4,7},{5,6},{6,5},{7,4},{8,11},{9,10},{10,... | collective-permute-start | bytes 196616 | tf_op jit(solution)/shard_map/ppermute | solution.py:23
  50.3 5.8 %collective-permute-start.20 = (f32[8,128]{1,0:T(8,128)S(1)}, f32[8,128]{1,0:T(8,128)S(1)}, u32[]{:S(2)}, u32[]{:S(2)}) collective-permute-start(f32[8,128]{1,0:T(8,128)S(1)} %get-tuple-element.31.mine), channel_id=1, source_target_pairs={{0,4},{4,0},{8,12},{12,8},{16,20},{20,16},{24,28},{28,24},{1,5},{5... | collective-permute-start | bytes 12296 | tf_op jit(solution)/shard_map/ppermute | solution.py:23
  50.4 15.4 %collective-permute-start.7 = (bf16[32,1024]{1,0:T(8,128)(2,1)S(1)}, bf16[32,1024]{1,0:T(8,128)(2,1)S(1)}, u32[]{:S(2)}, u32[]{:S(2)}) collective-permute-start(bf16[32,1024]{1,0:T(8,128)(2,1)S(1)} %get-tuple-element.26.refs_0_), channel_id=1, source_target_pairs={{0,1},{1,0},{2,3},{3,2},{4,5},{5,4},{6,7},{7,6},{8,9},{9,8},{10,11... | collective-permute-start | bytes 196616 | tf_op jit(solution)/shard_map/ppermute | solution.py:23
  54.0 11.8 %collective-permute-start.8 = (bf16[32,1024]{1,0:T(8,128)(2,1)S(1)}, bf16[32,1024]{1,0:T(8,128)(2,1)S(1)}, u32[]{:S(2)}, u32[]{:S(2)}) collective-permute-start(bf16[32,1024]{1,0:T(8,128)(2,1)S(1)} %get-tuple-element.26.refs_0_), channel_id=1, source_target_pairs={{0,2},{1,3},{2,0},{3,1},{4,6},{5,7},{6,4},{7,5},{8,10},{9,11},{10,... | collective-permute-start | bytes 196616 | tf_op jit(solution)/shard_map/ppermute | solution.py:23
  56.1 9.6 %collective-permute-start.9 = (bf16[32,1024]{1,0:T(8,128)(2,1)S(1)}, bf16[32,1024]{1,0:T(8,128)(2,1)S(1)}, u32[]{:S(2)}, u32[]{:S(2)}) collective-permute-start(bf16[32,1024]{1,0:T(8,128)(2,1)S(1)} %get-tuple-element.26.refs_0_), channel_id=1, source_target_pairs={{0,3},{1,2},{2,1},{3,0},{4,7},{5,6},{6,5},{7,4},{8,11},{9,10},{10,... | collective-permute-start | bytes 196616 | tf_op jit(solution)/shard_map/ppermute | solution.py:23
  57.6 3.6 %collective-permute-start.21 = (f32[8,128]{1,0:T(8,128)S(1)}, f32[8,128]{1,0:T(8,128)S(1)}, u32[]{:S(2)}, u32[]{:S(2)}) collective-permute-start(f32[8,128]{1,0:T(8,128)S(1)} %shard_map.117.refs_8_), channel_id=1, source_target_pairs={{0,8},{4,12},{8,0},{12,4},{16,24},{20,28},{24,16},{28,20},{1,9},{5... | collective-permute-start | bytes 12296 | tf_op jit(solution)/shard_map/ppermute | solution.py:23
  58.2 3.6 %collective-permute-start.22 = (f32[8,128]{1,0:T(8,128)S(1)}, f32[8,128]{1,0:T(8,128)S(1)}, u32[]{:S(2)}, u32[]{:S(2)}) collective-permute-start(f32[8,128]{1,0:T(8,128)S(1)} %shard_map.117.refs_8_), channel_id=1, source_target_pairs={{0,16},{4,20},{8,24},{12,28},{16,0},{20,4},{24,8},{28,12},{1,17},{... | collective-permute-start | bytes 12296 | tf_op jit(solution)/shard_map/ppermute | solution.py:23
  61.2 4.5 %collective-permute-start.23 = (f32[8,128]{1,0:T(8,128)S(1)}, f32[8,128]{1,0:T(8,128)S(1)}, u32[]{:S(2)}, u32[]{:S(2)}) collective-permute-start(f32[8,128]{1,0:T(8,128)S(1)} %shard_map.117.refs_8_), channel_id=1, source_target_pairs={{0,24},{4,28},{8,16},{12,20},{16,8},{20,12},{24,0},{28,4},{1,25},{... | collective-permute-start | bytes 12296 | tf_op jit(solution)/shard_map/ppermute | solution.py:23
  70.5 4.5 %collective-permute-start.24 = (bf16[64,2048]{1,0:T(8,128)(2,1)S(1)}, bf16[64,2048]{1,0:T(8,128)(2,1)S(1)}, u32[]{:S(2)}, u32[]{:S(2)}) collective-permute-start(bf16[64,2048]{1,0:T(8,128)(2,1)S(1)} %get-tuple-element.33), channel_id=1, source_target_pairs={{0,4},{4,0},{8,12},{12,8},{16,20},{20,16},{24,28},{28,24},{1,5},{5... | collective-permute-start | bytes 786440 | tf_op jit(solution)/shard_map/ppermute | solution.py:23
  70.6 5.8 %collective-permute-start.28 = (bf16[256,128]{1,0:T(8,128)(2,1)S(1)}, bf16[256,128]{1,0:T(8,128)(2,1)S(1)}, u32[]{:S(2)}, u32[]{:S(2)}) collective-permute-start(bf16[256,128]{1,0:T(8,128)(2,1)S(1)} %get-tuple-element.39), channel_id=1, source_target_pairs={{0,1},{1,0},{2,3},{3,2},{4,5},{5,4},{6,7},{7,6},{8,9},{9,8},{10,11... | collective-permute-start | bytes 196616 | tf_op jit(solution)/shard_map/ppermute | solution.py:23
  71.1 7.5 %collective-permute-start.29 = (bf16[256,128]{1,0:T(8,128)(2,1)S(1)}, bf16[256,128]{1,0:T(8,128)(2,1)S(1)}, u32[]{:S(2)}, u32[]{:S(2)}) collective-permute-start(bf16[256,128]{1,0:T(8,128)(2,1)S(1)} %get-tuple-element.40), channel_id=1, source_target_pairs={{0,2},{1,3},{2,0},{3,1},{4,6},{5,7},{6,4},{7,5},{8,10},{9,11},{10,... | collective-permute-start | bytes 196616 | tf_op jit(solution)/shard_map/ppermute | solution.py:23
  73.6 6.1 %collective-permute-start.30 = (bf16[256,128]{1,0:T(8,128)(2,1)S(1)}, bf16[256,128]{1,0:T(8,128)(2,1)S(1)}, u32[]{:S(2)}, u32[]{:S(2)}) collective-permute-start(bf16[256,128]{1,0:T(8,128)(2,1)S(1)} %get-tuple-element.41), channel_id=1, source_target_pairs={{0,3},{1,2},{2,1},{3,0},{4,7},{5,6},{6,5},{7,4},{8,11},{9,10},{10,... | collective-permute-start | bytes 196616 | tf_op jit(solution)/shard_map/ppermute | solution.py:23
  75.1 4.9 %collective-permute-start.25 = (bf16[16,2048]{1,0:T(8,128)(2,1)S(1)}, bf16[16,2048]{1,0:T(8,128)(2,1)S(1)}, u32[]{:S(2)}, u32[]{:S(2)}) collective-permute-start(bf16[16,2048]{1,0:T(8,128)(2,1)S(1)} %get-tuple-element.35), channel_id=1, source_target_pairs={{0,8},{4,12},{8,0},{12,4},{16,24},{20,28},{24,16},{28,20},{1,9},{5... | collective-permute-start | bytes 196616 | tf_op jit(solution)/shard_map/ppermute | solution.py:23
  75.7 4.7 %collective-permute-start.26 = (bf16[16,2048]{1,0:T(8,128)(2,1)S(1)}, bf16[16,2048]{1,0:T(8,128)(2,1)S(1)}, u32[]{:S(2)}, u32[]{:S(2)}) collective-permute-start(bf16[16,2048]{1,0:T(8,128)(2,1)S(1)} %get-tuple-element.36), channel_id=1, source_target_pairs={{0,16},{4,20},{8,24},{12,28},{16,0},{20,4},{24,8},{28,12},{1,17},{... | collective-permute-start | bytes 196616 | tf_op jit(solution)/shard_map/ppermute | solution.py:23
  76.4 5.2 %collective-permute-start.27 = (bf16[16,2048]{1,0:T(8,128)(2,1)S(1)}, bf16[16,2048]{1,0:T(8,128)(2,1)S(1)}, u32[]{:S(2)}, u32[]{:S(2)}) collective-permute-start(bf16[16,2048]{1,0:T(8,128)(2,1)S(1)} %get-tuple-element.37), channel_id=1, source_target_pairs={{0,24},{4,28},{8,16},{12,20},{16,8},{20,12},{24,0},{28,4},{1,25},{... | collective-permute-start | bytes 196616 | tf_op jit(solution)/shard_map/ppermute | solution.py:23

commit v3 on v2

--- a/solution.py
+++ b/solution.py
@@ -178,7 +178,7 @@
     index_slices, refs = refs[:peers], refs[peers:]
     totals, refs = refs[: len(offsets) + 1], refs[len(offsets) + 1 :]
     iq_a, iq_b, w_a, w_b, index_keys, keys_t, keep, away = refs[:8]
-    dk_outs, (rows, prob, dk) = refs[8:-3], refs[-3:]
+    dk_outs, (rows, prob, dk, dk_rows) = refs[8:-4], refs[-4:]
     count, keys = prob.shape
     depth = keys_t.shape[0]
     heads = iq_a.shape[1] // depth
@@ -221,15 +221,16 @@
             part = slice((first + i) * depth, (first + i + 1) * depth)
             keep[:, part] = dq[i * count : i * count + half]
             away[:, part] = dq[i * count + half : (i + 1) * count].astype(BF16)
-        term = lax.dot_general(d_score, mine, (((0,), (0,)), ((), ())), preferred_element_type=F32)
+        term = lax.dot_general(mine, d_score, (((0,), (0,)), ((), ())), preferred_element_type=F32)
         if first == 0:
             dk[...] = term
         else:
             dk[...] += term
+    dk_rows[...] = jnp.transpose(dk[...]) * scale
     size = keys // peers
     for k, out in enumerate(dk_outs):
         start = pl.multiple_of(jnp.bitwise_xor(info[1], k) * size, size)
-        out[...] = (dk[pl.ds(start, size), :] * scale).astype(out.dtype)
+        out[...] = dk_rows[pl.ds(start, size), :].astype(out.dtype)
 
 
 def fold_kernel(keep, other, own, *outs):
@@ -383,6 +384,7 @@
         scratch_shapes=[
             pltpu.VMEM((index_heads * count, depth), BF16),
             pltpu.VMEM((count, keys), F32),
+            pltpu.VMEM((depth, keys), F32),
             pltpu.VMEM((keys, depth), F32),
         ],
     )(

time: 82.6 us -> 81.8 us (level)
  no operation moved by 1% of the time
where the time goes in v3:
time: 81.8 us; the launch traced here: 81.5 us
  starting transfers between devices  38.3 us (47%)
  Pallas kernels  17.7 us (22%)
  waiting for transfers between devices  16.6 us (20%)
  local copies, waits for them, and re-layouts  5.83 us (7%)
  between operations  1.72 us (2%)
  other arithmetic  1.33 us (2%)
    ppermute x31, starting transfers between devices, send(): return lax.ppermute(array, axis, [(i, i ^ offset) for i in range(size)])  38.3 us
    ppermute x31, waiting for transfers between devices, send(): return lax.ppermute(array, axis, [(i, i ^ offset) for i in range(size)])  16.6 us
    pallas_call x1, Pallas kernels, body(): call(functools.partial(prob_kernel, width ** (-0.5)), [jax.ShapeDtypeStru...  10.3 us
    pallas_call x1, Pallas kernels, body(): call(functools.partial(grad_kernel, loss_scale, chunk, peers, evens), [ja...  3.91 us
    pallas_call x1, Pallas kernels, body(): call(logit_kernel, [jax.ShapeDtypeStruct((part_rows, keys), F32)] * peers...  1.83 us
  transfers between devices with their start and end apart: 31, of which 13 were waited for; matrix products, arithmetic and copies ran while one was open for 6% of the time, Pallas kernels for 16%

profile of v3, /device:TPU:0, one launch (start us, length us, event | category | flops | bytes accessed | tf_op | source)
XLA Modules:
  0.0 81.5 jit_solution(1112828835202860046)
XLA Ops:
  0.6 0.9 %slice.15 = bf16[16,32,128]{2,1,0:T(8,128)(2,1)S(1)} slice(bf16[16,32,192]{2,1,0:T(8,128)(2,1)} %param.10), slice={[0:16], [0:32], [0:128]} | slice | bytes 262144 | tf_op jit(solution)/shard_map/slice | solution.py:295
  1.6 0.9 %slice.16 = bf16[16,32,64]{2,1,0:T(8,128)(2,1)S(1)} slice(bf16[16,32,192]{2,1,0:T(8,128)(2,1)} %param.10), slice={[0:16], [0:32], [128:192]} | slice | bytes 131072 | tf_op jit(solution)/shard_map/slice | solution.py:295
  2.7 3.0 %collective-permute-start = (bf16[16,6144]{1,0:T(8,128)(2,1)S(1)}, bf16[16,6144]{1,0:T(8,128)(2,1)S(1)}, u32[]{:S(2)}, u32[]{:S(2)}) collective-permute-start(bf16[16,6144]{1,0:T(8,128)(2,1)S(1)} %constant_dynamic-update-slice_fusion), channel_id=1, source_target_pairs={{0,8},{4,12},{8,0},{12,4},{16,24},{20,28},{24,16},{28,20},{1,9},{5... | collective-permute-start | bytes 589832 | tf_op jit(solution)/shard_map/ppermute | solution.py:23
  5.8 1.5 %collective-permute-start.1 = (bf16[16,6144]{1,0:T(8,128)(2,1)S(1)}, bf16[16,6144]{1,0:T(8,128)(2,1)S(1)}, u32[]{:S(2)}, u32[]{:S(2)}) collective-permute-start(bf16[16,6144]{1,0:T(8,128)(2,1)S(1)} %constant_dynamic-update-slice_fusion), channel_id=1, source_target_pairs={{0,16},{4,20},{8,24},{12,28},{16,0},{20,4},{24,8},{28,12},{1,17},{... | collective-permute-start | bytes 589832 | tf_op jit(solution)/shard_map/ppermute | solution.py:23
  7.3 0.9 %copy.39 = bf16[2,8,16,128]{3,1,2,0:T(8,128)(2,1)S(1)} copy(bf16[2,8,16,128]{3,2,1,0:T(8,128)(2,1)} %bitcast.46) | data formatting | bytes 131072
  8.2 0.7 pad.9
  8.9 2.0 %collective-permute-start.10 = (bf16[16,2176]{1,0:T(8,128)(2,1)S(1)}, bf16[16,2176]{1,0:T(8,128)(2,1)S(1)}, u32[]{:S(2)}, u32[]{:S(2)}) collective-permute-start(bf16[16,2176]{1,0:T(8,128)(2,1)S(1)} %pad_maximum_fusion.2), channel_id=1, source_target_pairs={{0,8},{4,12},{8,0},{12,4},{16,24},{20,28},{24,16},{28,20},{1,9},{5... | collective-permute-start | bytes 208904 | tf_op jit(solution)/shard_map/ppermute | solution.py:23
  10.9 1.5 %collective-permute-start.11 = (bf16[16,2176]{1,0:T(8,128)(2,1)S(1)}, bf16[16,2176]{1,0:T(8,128)(2,1)S(1)}, u32[]{:S(2)}, u32[]{:S(2)}) collective-permute-start(bf16[16,2176]{1,0:T(8,128)(2,1)S(1)} %pad_maximum_fusion.2), channel_id=1, source_target_pairs={{0,16},{4,20},{8,24},{12,28},{16,0},{20,4},{24,8},{28,12},{1,17},{... | collective-permute-start | bytes 208904 | tf_op jit(solution)/shard_map/ppermute | solution.py:23
  12.4 0.7 convert_element_type.10
  13.3 0.2 concatenate.79
  13.7 0.2 concatenate.78
  16.2 0.8 collective-permute-done.1
  17.1 0.7 collective-permute-done.11
  17.8 3.5 %collective-permute-done.12 = bf16[16,2176]{1,0:T(8,128)(2,1)S(1)} collective-permute-done((bf16[16,2176]{1,0:T(8,128)(2,1)S(1)}, bf16[16,2176]{1,0:T(8,128)(2,1)S(1)}, u32[]{:S(2)}, u32[]{:S(2)}) %collective-permute-start.12) | collective-permute-done | bytes 69664 | tf_op jit(solution)/shard_map/ppermute | solution.py:23
  22.0 1.0 %collective-permute-done.13.iq_b.w_b.refs_13_.refs_15_ = bf16[64,2176]{1,0:T(8,128)(2,1)S(1)} collective-permute-done((bf16[64,2176]{1,0:T(8,128)(2,1)S(1)}, bf16[64,2176]{1,0:T(8,128)(2,1)S(1)}, u32[]{:S(2)}, u32[]{:S(2)}) %collective-permute-start.13) | collective-permute-done | bytes 278560 | tf_op jit(solution)/shard_map/ppermute | solution.py:23
  23.0 1.8 %shard_map.115 = (f32[32,1024]{1,0:T(8,128)S(1)}, f32[32,1024]{1,0:T(8,128)S(1)}, f32[32,1024]{1,0:T(8,128)S(1)}, f32[32,1024]{1,0:T(8,128)S(1)}) custom-call(s32[2]{0:T(128)S(1)} %pad_add_fusion.info, bf16[64,2176]{1,0:T(8,128)(2,1)S(1)} %pad_maximum_fusion.1.iq_a.w_a.refs_12_.refs_14_, ...), custom_call_target="tpu_custom_call" | custom-call | tf_op jit(solution)/shard_map/pallas_call | solution.py:317
  24.8 1.6 %collective-permute-start.14 = (f32[32,1024]{1,0:T(8,128)S(1)}, f32[32,1024]{1,0:T(8,128)S(1)}, u32[]{:S(2)}, u32[]{:S(2)}) collective-permute-start(f32[32,1024]{1,0:T(8,128)S(1)} %get-tuple-element.28), channel_id=1, source_target_pairs={{0,1},{1,0},{2,3},{3,2},{4,5},{5,4},{6,7},{7,6},{8,9},{9,8},{10,11... | collective-permute-start | bytes 393224 | tf_op jit(solution)/shard_map/ppermute | solution.py:23
  26.5 2.6 %collective-permute-start.15 = (f32[32,1024]{1,0:T(8,128)S(1)}, f32[32,1024]{1,0:T(8,128)S(1)}, u32[]{:S(2)}, u32[]{:S(2)}) collective-permute-start(f32[32,1024]{1,0:T(8,128)S(1)} %get-tuple-element.29), channel_id=1, source_target_pairs={{0,2},{1,3},{2,0},{3,1},{4,6},{5,7},{6,4},{7,5},{8,10},{9,11},{10,... | collective-permute-start | bytes 393224 | tf_op jit(solution)/shard_map/ppermute | solution.py:23
  29.1 0.2 collective-permute-start.16
  29.4 10.3 %shard_map.113 = (bf16[32,1152]{1,0:T(8,128)(2,1)S(1)}, bf16[32,1152]{1,0:T(8,128)(2,1)S(1)}, bf16[32,1152]{1,0:T(8,128)(2,1)S(1)}, bf16[32,1152]{1,0:T(8,128)(2,1)S(1)}) custom-call(s32[2]{0:T(128)S(1)} %pad_add_fusion.info, bf16[64,6144]{1,0:T(8,128)(2,1)S(1)} %pad_maximum_fusion.na.ra, bf16[64,6144]{1,0:T(8,128)(2,1)S(1)} %collective-permute-done.3.nb.rb, ...), custom_call_target="tpu_custom_call" | custom-call | tf_op jit(solution)/shard_map/pallas_call | solution.py:336
  39.8 0.7 collective-permute-start.4
  40.5 3.5 %collective-permute-start.5 = (bf16[32,1152]{1,0:T(8,128)(2,1)S(1)}, bf16[32,1152]{1,0:T(8,128)(2,1)S(1)}, u32[]{:S(2)}, u32[]{:S(2)}) collective-permute-start(bf16[32,1152]{1,0:T(8,128)(2,1)S(1)} %get-tuple-element.24), channel_id=1, source_target_pairs={{0,2},{1,3},{2,0},{3,1},{4,6},{5,7},{6,4},{7,5},{8,10},{9,11},{10,... | collective-permute-start | bytes 221192 | tf_op jit(solution)/shard_map/ppermute | solution.py:23
  44.0 0.2 collective-permute-start.6
  44.2 0.6 shard_map.116.refs_4_
  44.9 0.4 collective-permute-start.17
  45.3 3.8 %collective-permute-start.18 = (bf16[32,1024]{1,0:T(8,128)(2,1)S(1)}, bf16[32,1024]{1,0:T(8,128)(2,1)S(1)}, u32[]{:S(2)}, u32[]{:S(2)}) collective-permute-start(bf16[32,1024]{1,0:T(8,128)(2,1)S(1)} %shard_map.116.refs_4_), channel_id=1, source_target_pairs={{0,2},{1,3},{2,0},{3,1},{4,6},{5,7},{6,4},{7,5},{8,10},{9,11},{10,... | collective-permute-start | bytes 196616 | tf_op jit(solution)/shard_map/ppermute | solution.py:23
  49.1 0.2 collective-permute-start.19
  49.3 0.9 %collective-permute-done.5.refs_2_ = bf16[32,1152]{1,0:T(8,128)(2,1)S(1)} collective-permute-done((bf16[32,1152]{1,0:T(8,128)(2,1)S(1)}, bf16[32,1152]{1,0:T(8,128)(2,1)S(1)}, u32[]{:S(2)}, u32[]{:S(2)}) %collective-permute-start.5) | collective-permute-done | bytes 73760 | tf_op jit(solution)/shard_map/ppermute | solution.py:23
  50.4 3.6 %collective-permute-start.7 = (bf16[32,1024]{1,0:T(8,128)(2,1)S(1)}, bf16[32,1024]{1,0:T(8,128)(2,1)S(1)}, u32[]{:S(2)}, u32[]{:S(2)}) collective-permute-start(bf16[32,1024]{1,0:T(8,128)(2,1)S(1)} %get-tuple-element.26.refs_0_), channel_id=1, source_target_pairs={{0,1},{1,0},{2,3},{3,2},{4,5},{5,4},{6,7},{7,6},{8,9},{9,8},{10,11... | collective-permute-start | bytes 196616 | tf_op jit(solution)/shard_map/ppermute | solution.py:23
  54.0 2.1 %collective-permute-start.8 = (bf16[32,1024]{1,0:T(8,128)(2,1)S(1)}, bf16[32,1024]{1,0:T(8,128)(2,1)S(1)}, u32[]{:S(2)}, u32[]{:S(2)}) collective-permute-start(bf16[32,1024]{1,0:T(8,128)(2,1)S(1)} %get-tuple-element.26.refs_0_), channel_id=1, source_target_pairs={{0,2},{1,3},{2,0},{3,1},{4,6},{5,7},{6,4},{7,5},{8,10},{9,11},{10,... | collective-permute-start | bytes 196616 | tf_op jit(solution)/shard_map/ppermute | solution.py:23
  56.1 1.4 %collective-permute-start.9 = (bf16[32,1024]{1,0:T(8,128)(2,1)S(1)}, bf16[32,1024]{1,0:T(8,128)(2,1)S(1)}, u32[]{:S(2)}, u32[]{:S(2)}) collective-permute-start(bf16[32,1024]{1,0:T(8,128)(2,1)S(1)} %get-tuple-element.26.refs_0_), channel_id=1, source_target_pairs={{0,3},{1,2},{2,1},{3,0},{4,7},{5,6},{6,5},{7,4},{8,11},{9,10},{10,... | collective-permute-start | bytes 196616 | tf_op jit(solution)/shard_map/ppermute | solution.py:23
  57.6 0.5 collective-permute-start.21
  58.2 0.5 collective-permute-start.22
  58.7 2.6 %collective-permute-done.21.refs_9_ = f32[8,128]{1,0:T(8,128)S(1)} collective-permute-done((f32[8,128]{1,0:T(8,128)S(1)}, f32[8,128]{1,0:T(8,128)S(1)}, u32[]{:S(2)}, u32[]{:S(2)}) %collective-permute-start.21) | collective-permute-done | bytes 4128 | tf_op jit(solution)/shard_map/ppermute | solution.py:23
  61.2 0.5 collective-permute-start.23
  61.8 4.0 %collective-permute-done.23.refs_11_ = f32[8,128]{1,0:T(8,128)S(1)} collective-permute-done((f32[8,128]{1,0:T(8,128)S(1)}, f32[8,128]{1,0:T(8,128)S(1)}, u32[]{:S(2)}, u32[]{:S(2)}) %collective-permute-start.23) | collective-permute-done | bytes 4128 | tf_op jit(solution)/shard_map/ppermute | solution.py:23
  65.8 3.9 %shard_map.118 = (f32[64,2048]{1,0:T(8,128)S(1)}, bf16[64,2048]{1,0:T(8,128)(2,1)S(1)}, f32[256,128]{1,0:T(8,128)S(1)}, bf16[256,128]{1,0:T(8,128)(2,1)S(1)}, bf...) custom-call(s32[2]{0:T(128)S(1)} %pad_add_fusion.info, bf16[32,1024]{1,0:T(8,128)(2,1)S(1)} %get-tuple-element.26.refs_0_, ...), custom_call_target="tpu_custom_call" | custom-call | tf_op jit(solution)/shard_map/pallas_call | solution.py:371
  69.8 0.6 collective-permute-start.28
  70.3 2.4 %collective-permute-start.29 = (bf16[256,128]{1,0:T(8,128)(2,1)S(1)}, bf16[256,128]{1,0:T(8,128)(2,1)S(1)}, u32[]{:S(2)}, u32[]{:S(2)}) collective-permute-start(bf16[256,128]{1,0:T(8,128)(2,1)S(1)} %get-tuple-element.40), channel_id=1, source_target_pairs={{0,2},{1,3},{2,0},{3,1},{4,6},{5,7},{6,4},{7,5},{8,10},{9,11},{10,... | collective-permute-start | bytes 196616 | tf_op jit(solution)/shard_map/ppermute | solution.py:23
  72.8 1.4 %collective-permute-start.30 = (bf16[256,128]{1,0:T(8,128)(2,1)S(1)}, bf16[256,128]{1,0:T(8,128)(2,1)S(1)}, u32[]{:S(2)}, u32[]{:S(2)}) collective-permute-start(bf16[256,128]{1,0:T(8,128)(2,1)S(1)} %get-tuple-element.41), channel_id=1, source_target_pairs={{0,3},{1,2},{2,1},{3,0},{4,7},{5,6},{6,5},{7,4},{8,11},{9,10},{10,... | collective-permute-start | bytes 196616 | tf_op jit(solution)/shard_map/ppermute | solution.py:23
  74.3 0.6 collective-permute-start.25
  74.9 0.5 collective-permute-start.26
  75.6 2.3 %collective-permute-start.27 = (bf16[16,2048]{1,0:T(8,128)(2,1)S(1)}, bf16[16,2048]{1,0:T(8,128)(2,1)S(1)}, u32[]{:S(2)}, u32[]{:S(2)}) collective-permute-start(bf16[16,2048]{1,0:T(8,128)(2,1)S(1)} %get-tuple-element.37), channel_id=1, source_target_pairs={{0,24},{4,28},{8,16},{12,20},{16,8},{20,12},{24,0},{28,4},{1,25},{... | collective-permute-start | bytes 196616 | tf_op jit(solution)/shard_map/ppermute | solution.py:23
  77.8 1.0 %collective-permute-done.30.refs_7_ = bf16[256,128]{1,0:T(8,128)(2,1)S(1)} collective-permute-done((bf16[256,128]{1,0:T(8,128)(2,1)S(1)}, bf16[256,128]{1,0:T(8,128)(2,1)S(1)}, u32[]{:S(2)}, u32[]{:S(2)}) %collective-permute-start.30) | collective-permute-done | bytes 65568 | tf_op jit(solution)/shard_map/ppermute | solution.py:23
  78.9 0.3 collective-permute-done.25.refs_1_
  79.2 0.4 collective-permute-done.26.refs_2_
  79.6 1.1 %collective-permute-done.27.refs_3_ = bf16[16,2048]{1,0:T(8,128)(2,1)S(1)} collective-permute-done((bf16[16,2048]{1,0:T(8,128)(2,1)S(1)}, bf16[16,2048]{1,0:T(8,128)(2,1)S(1)}, u32[]{:S(2)}, u32[]{:S(2)}) %collective-permute-start.27) | collective-permute-done | bytes 65568 | tf_op jit(solution)/shard_map/ppermute | solution.py:23
  80.7 0.8 shard_map.120
  (65 shorter events, 3.6 us)
Async XLA Ops:
  0.6 12.8 %copy-start.3 = (f32[128]{0:T(128)S(1)}, f32[128]{0:T(128)}, u32[]{:S(2)}) copy-start(f32[128]{0:T(128)} %param.17) | copy-start | bytes 1540
  0.6 14.1 %copy-start.2 = (f32[128,32]{0,1:T(8,128)S(1)}, f32[128,32]{0,1:T(8,128)}, u32[]{:S(2)}) copy-start(f32[128,32]{0,1:T(8,128)} %param.13) | copy-start | bytes 49156
  2.7 13.3 %collective-permute-start = (bf16[16,6144]{1,0:T(8,128)(2,1)S(1)}, bf16[16,6144]{1,0:T(8,128)(2,1)S(1)}, u32[]{:S(2)}, u32[]{:S(2)}) collective-permute-start(bf16[16,6144]{1,0:T(8,128)(2,1)S(1)} %constant_dynamic-update-slice_fusion), channel_id=1, source_target_pairs={{0,8},{4,12},{8,0},{12,4},{16,24},{20,28},{24,16},{28,20},{1,9},{5... | collective-permute-start | bytes 589832 | tf_op jit(solution)/shard_map/ppermute | solution.py:23
  5.8 11.2 %collective-permute-start.1 = (bf16[16,6144]{1,0:T(8,128)(2,1)S(1)}, bf16[16,6144]{1,0:T(8,128)(2,1)S(1)}, u32[]{:S(2)}, u32[]{:S(2)}) collective-permute-start(bf16[16,6144]{1,0:T(8,128)(2,1)S(1)} %constant_dynamic-update-slice_fusion), channel_id=1, source_target_pairs={{0,16},{4,20},{8,24},{12,28},{16,0},{20,4},{24,8},{28,12},{1,17},{... | collective-permute-start | bytes 589832 | tf_op jit(solution)/shard_map/ppermute | solution.py:23
  7.3 9.7 %collective-permute-start.2 = (bf16[16,6144]{1,0:T(8,128)(2,1)S(1)}, bf16[16,6144]{1,0:T(8,128)(2,1)S(1)}, u32[]{:S(2)}, u32[]{:S(2)}) collective-permute-start(bf16[16,6144]{1,0:T(8,128)(2,1)S(1)} %constant_dynamic-update-slice_fusion), channel_id=1, source_target_pairs={{0,24},{4,28},{8,16},{12,20},{16,8},{20,12},{24,0},{28,4},{1,25},{... | collective-permute-start | bytes 589832 | tf_op jit(solution)/shard_map/ppermute | solution.py:23
  8.9 8.2 %collective-permute-start.10 = (bf16[16,2176]{1,0:T(8,128)(2,1)S(1)}, bf16[16,2176]{1,0:T(8,128)(2,1)S(1)}, u32[]{:S(2)}, u32[]{:S(2)}) collective-permute-start(bf16[16,2176]{1,0:T(8,128)(2,1)S(1)} %pad_maximum_fusion.2), channel_id=1, source_target_pairs={{0,8},{4,12},{8,0},{12,4},{16,24},{20,28},{24,16},{28,20},{1,9},{5... | collective-permute-start | bytes 208904 | tf_op jit(solution)/shard_map/ppermute | solution.py:23
  10.9 6.9 %collective-permute-start.11 = (bf16[16,2176]{1,0:T(8,128)(2,1)S(1)}, bf16[16,2176]{1,0:T(8,128)(2,1)S(1)}, u32[]{:S(2)}, u32[]{:S(2)}) collective-permute-start(bf16[16,2176]{1,0:T(8,128)(2,1)S(1)} %pad_maximum_fusion.2), channel_id=1, source_target_pairs={{0,16},{4,20},{8,24},{12,28},{16,0},{20,4},{24,8},{28,12},{1,17},{... | collective-permute-start | bytes 208904 | tf_op jit(solution)/shard_map/ppermute | solution.py:23
  15.2 6.5 %copy-start = (bf16[1024,128]{1,0:T(8,128)(2,1)S(1)}, bf16[1024,128]{1,0:T(8,128)(2,1)}, u32[]{:S(2)}) copy-start(bf16[1024,128]{1,0:T(8,128)(2,1)} %refs_16_.1) | copy-start | bytes 786436
  16.1 5.3 %collective-permute-start.12 = (bf16[16,2176]{1,0:T(8,128)(2,1)S(1)}, bf16[16,2176]{1,0:T(8,128)(2,1)S(1)}, u32[]{:S(2)}, u32[]{:S(2)}) collective-permute-start(bf16[16,2176]{1,0:T(8,128)(2,1)S(1)} %pad_maximum_fusion.2), channel_id=1, source_target_pairs={{0,24},{4,28},{8,16},{12,20},{16,8},{20,12},{24,0},{28,4},{1,25},{... | collective-permute-start | bytes 208904 | tf_op jit(solution)/shard_map/ppermute | solution.py:23
  17.0 12.4 %collective-permute-start.3 = (bf16[64,6144]{1,0:T(8,128)(2,1)S(1)}, bf16[64,6144]{1,0:T(8,128)(2,1)S(1)}, u32[]{:S(2)}, u32[]{:S(2)}) collective-permute-start(bf16[64,6144]{1,0:T(8,128)(2,1)S(1)} %pad_maximum_fusion.na.ra), channel_id=1, source_target_pairs={{0,4},{4,0},{8,12},{12,8},{16,20},{20,16},{24,28},{28,24},{1,5},{5... | collective-permute-start | bytes 2359304 | tf_op jit(solution)/shard_map/ppermute | solution.py:23
  21.4 1.6 %collective-permute-start.13 = (bf16[64,2176]{1,0:T(8,128)(2,1)S(1)}, bf16[64,2176]{1,0:T(8,128)(2,1)S(1)}, u32[]{:S(2)}, u32[]{:S(2)}) collective-permute-start(bf16[64,2176]{1,0:T(8,128)(2,1)S(1)} %pad_maximum_fusion.1.iq_a.w_a.refs_12_.refs_14_), channel_id=1, source_target_pairs={{0,4},{4,0},{8,12},{12,8},{16,20},{20,16},{24,28},{28,24},{1,5},{5... | collective-permute-start | bytes 835592 | tf_op jit(solution)/shard_map/ppermute | solution.py:23
  21.9 7.4 %copy-start.1 = (bf16[1024,576]{0,1:T(8,128)(2,1)S(1)}, bf16[1024,576]{0,1:T(8,128)(2,1)}, u32[]{:S(2)}) copy-start(bf16[1024,576]{0,1:T(8,128)(2,1)} %param.12) | copy-start | bytes 3538948
  24.8 19.2 %collective-permute-start.14 = (f32[32,1024]{1,0:T(8,128)S(1)}, f32[32,1024]{1,0:T(8,128)S(1)}, u32[]{:S(2)}, u32[]{:S(2)}) collective-permute-start(f32[32,1024]{1,0:T(8,128)S(1)} %get-tuple-element.28), channel_id=1, source_target_pairs={{0,1},{1,0},{2,3},{3,2},{4,5},{5,4},{6,7},{7,6},{8,9},{9,8},{10,11... | collective-permute-start | bytes 393224 | tf_op jit(solution)/shard_map/ppermute | solution.py:23
  26.5 17.7 %collective-permute-start.15 = (f32[32,1024]{1,0:T(8,128)S(1)}, f32[32,1024]{1,0:T(8,128)S(1)}, u32[]{:S(2)}, u32[]{:S(2)}) collective-permute-start(f32[32,1024]{1,0:T(8,128)S(1)} %get-tuple-element.29), channel_id=1, source_target_pairs={{0,2},{1,3},{2,0},{3,1},{4,6},{5,7},{6,4},{7,5},{8,10},{9,11},{10,... | collective-permute-start | bytes 393224 | tf_op jit(solution)/shard_map/ppermute | solution.py:23
  29.1 15.1 %collective-permute-start.16 = (f32[32,1024]{1,0:T(8,128)S(1)}, f32[32,1024]{1,0:T(8,128)S(1)}, u32[]{:S(2)}, u32[]{:S(2)}) collective-permute-start(f32[32,1024]{1,0:T(8,128)S(1)} %get-tuple-element.30), channel_id=1, source_target_pairs={{0,3},{1,2},{2,1},{3,0},{4,7},{5,6},{6,5},{7,4},{8,11},{9,10},{10,... | collective-permute-start | bytes 393224 | tf_op jit(solution)/shard_map/ppermute | solution.py:23
  39.8 9.4 %collective-permute-start.4 = (bf16[32,1152]{1,0:T(8,128)(2,1)S(1)}, bf16[32,1152]{1,0:T(8,128)(2,1)S(1)}, u32[]{:S(2)}, u32[]{:S(2)}) collective-permute-start(bf16[32,1152]{1,0:T(8,128)(2,1)S(1)} %get-tuple-element.23), channel_id=1, source_target_pairs={{0,1},{1,0},{2,3},{3,2},{4,5},{5,4},{6,7},{7,6},{8,9},{9,8},{10,11... | collective-permute-start | bytes 221192 | tf_op jit(solution)/shard_map/ppermute | solution.py:23
  40.5 9.8 %collective-permute-start.5 = (bf16[32,1152]{1,0:T(8,128)(2,1)S(1)}, bf16[32,1152]{1,0:T(8,128)(2,1)S(1)}, u32[]{:S(2)}, u32[]{:S(2)}) collective-permute-start(bf16[32,1152]{1,0:T(8,128)(2,1)S(1)} %get-tuple-element.24), channel_id=1, source_target_pairs={{0,2},{1,3},{2,0},{3,1},{4,6},{5,7},{6,4},{7,5},{8,10},{9,11},{10,... | collective-permute-start | bytes 221192 | tf_op jit(solution)/shard_map/ppermute | solution.py:23
  44.0 6.3 %collective-permute-start.6 = (bf16[32,1152]{1,0:T(8,128)(2,1)S(1)}, bf16[32,1152]{1,0:T(8,128)(2,1)S(1)}, u32[]{:S(2)}, u32[]{:S(2)}) collective-permute-start(bf16[32,1152]{1,0:T(8,128)(2,1)S(1)} %get-tuple-element.25), channel_id=1, source_target_pairs={{0,3},{1,2},{2,1},{3,0},{4,7},{5,6},{6,5},{7,4},{8,11},{9,10},{10,... | collective-permute-start | bytes 221192 | tf_op jit(solution)/shard_map/ppermute | solution.py:23
  44.9 9.1 %collective-permute-start.17 = (bf16[32,1024]{1,0:T(8,128)(2,1)S(1)}, bf16[32,1024]{1,0:T(8,128)(2,1)S(1)}, u32[]{:S(2)}, u32[]{:S(2)}) collective-permute-start(bf16[32,1024]{1,0:T(8,128)(2,1)S(1)} %shard_map.116.refs_4_), channel_id=1, source_target_pairs={{0,1},{1,0},{2,3},{3,2},{4,5},{5,4},{6,7},{7,6},{8,9},{9,8},{10,11... | collective-permute-start | bytes 196616 | tf_op jit(solution)/shard_map/ppermute | solution.py:23
  45.3 12.4 %collective-permute-start.18 = (bf16[32,1024]{1,0:T(8,128)(2,1)S(1)}, bf16[32,1024]{1,0:T(8,128)(2,1)S(1)}, u32[]{:S(2)}, u32[]{:S(2)}) collective-permute-start(bf16[32,1024]{1,0:T(8,128)(2,1)S(1)} %shard_map.116.refs_4_), channel_id=1, source_target_pairs={{0,2},{1,3},{2,0},{3,1},{4,6},{5,7},{6,4},{7,5},{8,10},{9,11},{10,... | collective-permute-start | bytes 196616 | tf_op jit(solution)/shard_map/ppermute | solution.py:23
  49.1 9.1 %collective-permute-start.19 = (bf16[32,1024]{1,0:T(8,128)(2,1)S(1)}, bf16[32,1024]{1,0:T(8,128)(2,1)S(1)}, u32[]{:S(2)}, u32[]{:S(2)}) collective-permute-start(bf16[32,1024]{1,0:T(8,128)(2,1)S(1)} %shard_map.116.refs_4_), channel_id=1, source_target_pairs={{0,3},{1,2},{2,1},{3,0},{4,7},{5,6},{6,5},{7,4},{8,11},{9,10},{10,... | collective-permute-start | bytes 196616 | tf_op jit(solution)/shard_map/ppermute | solution.py:23
  50.3 5.8 %collective-permute-start.20 = (f32[8,128]{1,0:T(8,128)S(1)}, f32[8,128]{1,0:T(8,128)S(1)}, u32[]{:S(2)}, u32[]{:S(2)}) collective-permute-start(f32[8,128]{1,0:T(8,128)S(1)} %get-tuple-element.31.mine), channel_id=1, source_target_pairs={{0,4},{4,0},{8,12},{12,8},{16,20},{20,16},{24,28},{28,24},{1,5},{5... | collective-permute-start | bytes 12296 | tf_op jit(solution)/shard_map/ppermute | solution.py:23
  50.4 15.4 %collective-permute-start.7 = (bf16[32,1024]{1,0:T(8,128)(2,1)S(1)}, bf16[32,1024]{1,0:T(8,128)(2,1)S(1)}, u32[]{:S(2)}, u32[]{:S(2)}) collective-permute-start(bf16[32,1024]{1,0:T(8,128)(2,1)S(1)} %get-tuple-element.26.refs_0_), channel_id=1, source_target_pairs={{0,1},{1,0},{2,3},{3,2},{4,5},{5,4},{6,7},{7,6},{8,9},{9,8},{10,11... | collective-permute-start | bytes 196616 | tf_op jit(solution)/shard_map/ppermute | solution.py:23
  54.0 11.8 %collective-permute-start.8 = (bf16[32,1024]{1,0:T(8,128)(2,1)S(1)}, bf16[32,1024]{1,0:T(8,128)(2,1)S(1)}, u32[]{:S(2)}, u32[]{:S(2)}) collective-permute-start(bf16[32,1024]{1,0:T(8,128)(2,1)S(1)} %get-tuple-element.26.refs_0_), channel_id=1, source_target_pairs={{0,2},{1,3},{2,0},{3,1},{4,6},{5,7},{6,4},{7,5},{8,10},{9,11},{10,... | collective-permute-start | bytes 196616 | tf_op jit(solution)/shard_map/ppermute | solution.py:23
  56.1 9.6 %collective-permute-start.9 = (bf16[32,1024]{1,0:T(8,128)(2,1)S(1)}, bf16[32,1024]{1,0:T(8,128)(2,1)S(1)}, u32[]{:S(2)}, u32[]{:S(2)}) collective-permute-start(bf16[32,1024]{1,0:T(8,128)(2,1)S(1)} %get-tuple-element.26.refs_0_), channel_id=1, source_target_pairs={{0,3},{1,2},{2,1},{3,0},{4,7},{5,6},{6,5},{7,4},{8,11},{9,10},{10,... | collective-permute-start | bytes 196616 | tf_op jit(solution)/shard_map/ppermute | solution.py:23
  57.6 3.6 %collective-permute-start.21 = (f32[8,128]{1,0:T(8,128)S(1)}, f32[8,128]{1,0:T(8,128)S(1)}, u32[]{:S(2)}, u32[]{:S(2)}) collective-permute-start(f32[8,128]{1,0:T(8,128)S(1)} %shard_map.117.refs_8_), channel_id=1, source_target_pairs={{0,8},{4,12},{8,0},{12,4},{16,24},{20,28},{24,16},{28,20},{1,9},{5... | collective-permute-start | bytes 12296 | tf_op jit(solution)/shard_map/ppermute | solution.py:23
  58.2 3.6 %collective-permute-start.22 = (f32[8,128]{1,0:T(8,128)S(1)}, f32[8,128]{1,0:T(8,128)S(1)}, u32[]{:S(2)}, u32[]{:S(2)}) collective-permute-start(f32[8,128]{1,0:T(8,128)S(1)} %shard_map.117.refs_8_), channel_id=1, source_target_pairs={{0,16},{4,20},{8,24},{12,28},{16,0},{20,4},{24,8},{28,12},{1,17},{... | collective-permute-start | bytes 12296 | tf_op jit(solution)/shard_map/ppermute | solution.py:23
  61.2 4.5 %collective-permute-start.23 = (f32[8,128]{1,0:T(8,128)S(1)}, f32[8,128]{1,0:T(8,128)S(1)}, u32[]{:S(2)}, u32[]{:S(2)}) collective-permute-start(f32[8,128]{1,0:T(8,128)S(1)} %shard_map.117.refs_8_), channel_id=1, source_target_pairs={{0,24},{4,28},{8,16},{12,20},{16,8},{20,12},{24,0},{28,4},{1,25},{... | collective-permute-start | bytes 12296 | tf_op jit(solution)/shard_map/ppermute | solution.py:23
  69.7 4.5 %collective-permute-start.24 = (bf16[64,2048]{1,0:T(8,128)(2,1)S(1)}, bf16[64,2048]{1,0:T(8,128)(2,1)S(1)}, u32[]{:S(2)}, u32[]{:S(2)}) collective-permute-start(bf16[64,2048]{1,0:T(8,128)(2,1)S(1)} %get-tuple-element.33), channel_id=1, source_target_pairs={{0,4},{4,0},{8,12},{12,8},{16,20},{20,16},{24,28},{28,24},{1,5},{5... | collective-permute-start | bytes 786440 | tf_op jit(solution)/shard_map/ppermute | solution.py:23
  69.8 5.8 %collective-permute-start.28 = (bf16[256,128]{1,0:T(8,128)(2,1)S(1)}, bf16[256,128]{1,0:T(8,128)(2,1)S(1)}, u32[]{:S(2)}, u32[]{:S(2)}) collective-permute-start(bf16[256,128]{1,0:T(8,128)(2,1)S(1)} %get-tuple-element.39), channel_id=1, source_target_pairs={{0,1},{1,0},{2,3},{3,2},{4,5},{5,4},{6,7},{7,6},{8,9},{9,8},{10,11... | collective-permute-start | bytes 196616 | tf_op jit(solution)/shard_map/ppermute | solution.py:23
  70.3 7.5 %collective-permute-start.29 = (bf16[256,128]{1,0:T(8,128)(2,1)S(1)}, bf16[256,128]{1,0:T(8,128)(2,1)S(1)}, u32[]{:S(2)}, u32[]{:S(2)}) collective-permute-start(bf16[256,128]{1,0:T(8,128)(2,1)S(1)} %get-tuple-element.40), channel_id=1, source_target_pairs={{0,2},{1,3},{2,0},{3,1},{4,6},{5,7},{6,4},{7,5},{8,10},{9,11},{10,... | collective-permute-start | bytes 196616 | tf_op jit(solution)/shard_map/ppermute | solution.py:23
  72.8 6.1 %collective-permute-start.30 = (bf16[256,128]{1,0:T(8,128)(2,1)S(1)}, bf16[256,128]{1,0:T(8,128)(2,1)S(1)}, u32[]{:S(2)}, u32[]{:S(2)}) collective-permute-start(bf16[256,128]{1,0:T(8,128)(2,1)S(1)} %get-tuple-element.41), channel_id=1, source_target_pairs={{0,3},{1,2},{2,1},{3,0},{4,7},{5,6},{6,5},{7,4},{8,11},{9,10},{10,... | collective-permute-start | bytes 196616 | tf_op jit(solution)/shard_map/ppermute | solution.py:23
  74.3 5.0 %collective-permute-start.25 = (bf16[16,2048]{1,0:T(8,128)(2,1)S(1)}, bf16[16,2048]{1,0:T(8,128)(2,1)S(1)}, u32[]{:S(2)}, u32[]{:S(2)}) collective-permute-start(bf16[16,2048]{1,0:T(8,128)(2,1)S(1)} %get-tuple-element.35), channel_id=1, source_target_pairs={{0,8},{4,12},{8,0},{12,4},{16,24},{20,28},{24,16},{28,20},{1,9},{5... | collective-permute-start | bytes 196616 | tf_op jit(solution)/shard_map/ppermute | solution.py:23
  74.9 4.7 %collective-permute-start.26 = (bf16[16,2048]{1,0:T(8,128)(2,1)S(1)}, bf16[16,2048]{1,0:T(8,128)(2,1)S(1)}, u32[]{:S(2)}, u32[]{:S(2)}) collective-permute-start(bf16[16,2048]{1,0:T(8,128)(2,1)S(1)} %get-tuple-element.36), channel_id=1, source_target_pairs={{0,16},{4,20},{8,24},{12,28},{16,0},{20,4},{24,8},{28,12},{1,17},{... | collective-permute-start | bytes 196616 | tf_op jit(solution)/shard_map/ppermute | solution.py:23
  75.6 5.2 %collective-permute-start.27 = (bf16[16,2048]{1,0:T(8,128)(2,1)S(1)}, bf16[16,2048]{1,0:T(8,128)(2,1)S(1)}, u32[]{:S(2)}, u32[]{:S(2)}) collective-permute-start(bf16[16,2048]{1,0:T(8,128)(2,1)S(1)} %get-tuple-element.37), channel_id=1, source_target_pairs={{0,24},{4,28},{8,16},{12,20},{16,8},{20,12},{24,0},{28,4},{1,25},{... | collective-permute-start | bytes 196616 | tf_op jit(solution)/shard_map/ppermute | solution.py:23
